TPU v7x, 512 devices: a whole 4x8x8 slice. The times are simulated.
512 devices in a mesh: frame: 16 (over y, core), row: 32 (over x, z).
Axes of the slice: x: 4, y: 8, z: 8, core: 2. Of those that a mesh axis runs over, the one named last changes fastest.
Arguments:
- video_tail: bfloat16 [16, 32, 128, 256], P('frame', 'row'), may hold values from -6 to 6
- video_head: bfloat16 [32, 128, 256], P('row', 'frame'), may hold values from -6 to 6
- cotangent_tail: bfloat16 [16, 32, 128, 256], P('frame', 'row'), may hold values from -6 to 6
- cotangent_head: bfloat16 [32, 128, 256], P('row', 'frame'), may hold values from -6 to 6
- modulation: float32 [256], replicated, may hold values from 0.25 to 1.75
- conv_weight: bfloat16 [9, 256, 256], replicated, may hold values from -0.125 to 0.125
- conv_bias: float32 [256], replicated, may hold values from -3 to 3
- temporal_weight: bfloat16 [3, 256, 256], replicated, may hold values from -0.21875 to 0.21875
Outputs:
- grad_tail: bfloat16 [16, 32, 128, 256], P('frame', 'row')
- grad_head: bfloat16 [32, 128, 256], P('row', 'frame')
- grad_conv: float32 [9, 256, 256], P(None, 'row')
- grad_temporal: float32 [3, 256, 256], P(None, 'row')
- grad_vectors: float32 [2, 256], P(None, 'row')
All inputs are finite; a program needn't handle non-finite values.
Results may differ from a plain program's by a relative error of at most 0.0061.
Values may be sent and summed in bfloat16 or wider, within the bound.
A program may use at most 64 MiB of HBM per device.

v0:
```python
import math

import jax
import jax.numpy as jnp
from jax import lax
from jax.sharding import PartitionSpec as P


def padded_2(x, sides, width):
    for axis, dim in sides:
        count, length = (lax.axis_size(axis), x.shape[dim])
        up = [(i, (i + 1) % count) for i in range(count - 1)]
        down = [(j, i) for i, j in up]
        last = lax.slice_in_dim(x, length - width, length, axis=dim)
        first = lax.slice_in_dim(x, 0, width, axis=dim)
        before = lax.ppermute(last, axis, up)
        after = lax.ppermute(first, axis, down)
        x = jnp.concatenate([before, x, after], axis=dim)
    return x


def conv_frames(padded, kernel):
    count_frames, padded_rows, padded_cols, channels = padded.shape
    height = padded_rows - 2
    breadth = padded_cols - 2
    summed = jnp.zeros((count_frames * height * breadth, kernel.shape[2]), jnp.float32)
    for tap_index in range(9):
        tap_row = tap_index // 3
        tap_col = tap_index % 3
        window = padded[:, tap_row : tap_row + height, tap_col : tap_col + breadth].reshape(
            count_frames * height * breadth, channels
        )
        summed = summed + jnp.dot(window, kernel[tap_index], preferred_element_type=jnp.float32)
    return summed.reshape(count_frames, height, breadth, kernel.shape[2])


def weight_frames(padded, gradient):
    count_frames, height, breadth, channels = gradient.shape
    flattened = gradient.reshape(count_frames * height * breadth, channels)
    results = []
    for tap_index in range(9):
        tap_row = tap_index // 3
        tap_col = tap_index % 3
        window = padded[:, tap_row : tap_row + height, tap_col : tap_col + breadth].reshape(
            count_frames * height * breadth, padded.shape[3]
        )
        results.append(
            lax.dot_general(
                window, flattened, (((0,), (0,)), ((), ())), preferred_element_type=jnp.float32
            )
        )
    return jnp.stack(results)


def flipped(kernel):
    return jnp.transpose(kernel[::-1], (0, 2, 1))


def silu_slope(pre_act):
    sigmoid_val = jax.nn.sigmoid(pre_act)
    return sigmoid_val * (1.0 + pre_act * (1.0 - sigmoid_val))


def times_back(rows, kernel):
    return lax.dot_general(
        rows, kernel, (((1,), (1,)), ((), ())), preferred_element_type=jnp.float32
    )


def outer_sum(left, right):
    return lax.dot_general(
        left, right, (((0,), (0,)), ((), ())), preferred_element_type=jnp.float32
    )


def body(
    video_tail,
    video_head,
    cotangent_tail,
    cotangent_head,
    modulation,
    conv_weight,
    conv_bias,
    temporal_weight,
):
    frame_count = lax.axis_size("frame")
    row_count = lax.axis_size("row")
    local_frames, height, breadth, channels = video_tail.shape
    head_breadth = video_head.shape[1]
    norm_scale = 1.0 / math.sqrt((local_frames * frame_count + 1) * height * row_count * breadth)
    kernel_back = flipped(conv_weight)

    def modulate(frames):
        return (frames.astype(jnp.float32) * modulation).astype(jnp.bfloat16)

    def row_rim(frames):
        extended = padded_2(frames, (("row", 1),), 1)
        return jnp.pad(extended, ((0, 0), (0, 0), (1, 1), (0, 0)))

    def head_rim(piece):
        return padded_2(piece, (("frame", 1), ("row", 0)), 1)

    padded_head = head_rim(modulate(video_head))
    pre_head = conv_frames(padded_head[None], conv_weight)[0] + conv_bias
    padded_tail = row_rim(modulate(video_tail))
    pre_tail = conv_frames(padded_tail, conv_weight) + conv_bias
    act_tail = jax.nn.silu(pre_tail).astype(jnp.bfloat16)
    act_head = jax.nn.silu(pre_head).astype(jnp.bfloat16)
    act_pos, cot_pos = (
        lax.all_to_all(act_tail, "frame", split_axis=2, concat_axis=0, tiled=True),
        lax.all_to_all(cotangent_tail, "frame", split_axis=2, concat_axis=0, tiled=True),
    )
    act_seq = jnp.concatenate([act_head[None], act_pos], axis=0)
    cot_seq = jnp.concatenate([cotangent_head[None], cot_pos], axis=0)
    seq_len = act_seq.shape[0]
    positions = height * head_breadth
    act_rows = act_seq.reshape(seq_len, positions, channels)
    cot_rows = cot_seq.reshape(seq_len, positions, channels)
    dgrad = jnp.zeros((seq_len * positions, channels), jnp.float32)
    temporal_terms = []
    for lag_index in range(3):
        ahead = jnp.concatenate(
            [cot_rows[lag_index:], jnp.zeros((lag_index, positions, channels), jnp.bfloat16)],
            axis=0,
        ).reshape(seq_len * positions, channels)
        behind = jnp.concatenate(
            [
                jnp.zeros((lag_index, positions, channels), jnp.bfloat16),
                act_rows[: seq_len - lag_index],
            ],
            axis=0,
        ).reshape(seq_len * positions, channels)
        dgrad = dgrad + times_back(ahead, temporal_weight[lag_index])
        temporal_terms.append(outer_sum(behind, cot_rows.reshape(seq_len * positions, channels)))
    act_grad = dgrad.astype(jnp.bfloat16).reshape(seq_len, height, head_breadth, channels)
    tail_act_grad = lax.all_to_all(act_grad[1:], "frame", split_axis=0, concat_axis=2, tiled=True)
    head_act_grad = act_grad[0]
    pre_grad_tail = (tail_act_grad.astype(jnp.float32) * silu_slope(pre_tail)).astype(jnp.bfloat16)
    pre_grad_head = (head_act_grad.astype(jnp.float32) * silu_slope(pre_head)).astype(jnp.bfloat16)
    mod_head = conv_frames(head_rim(pre_grad_head)[None], kernel_back)[0]
    mod_tail = conv_frames(row_rim(pre_grad_tail), kernel_back)
    grad_tail = (cotangent_tail.astype(jnp.float32) + modulation * mod_tail).astype(jnp.bfloat16)
    grad_head = (cotangent_head.astype(jnp.float32) + modulation * mod_head).astype(jnp.bfloat16)
    kernel_terms = weight_frames(padded_tail, pre_grad_tail) + weight_frames(
        padded_head[None], pre_grad_head[None]
    )
    scale_terms = jnp.sum(video_tail.astype(jnp.float32) * mod_tail, axis=(0, 1, 2)) + jnp.sum(
        video_head.astype(jnp.float32) * mod_head, axis=(0, 1)
    )
    bias_terms = jnp.sum(pre_grad_tail.astype(jnp.float32), axis=(0, 1, 2)) + jnp.sum(
        pre_grad_head.astype(jnp.float32), axis=(0, 1)
    )
    kernel_sum = kernel_terms * norm_scale
    temporal_sum = jnp.stack(temporal_terms) * norm_scale
    vector_sum = jnp.stack([scale_terms, bias_terms]) * norm_scale
    summed = lax.psum((kernel_sum, temporal_sum, vector_sum), ("frame", "row"))
    share_rows = channels // row_count
    first_row = lax.axis_index("row") * share_rows
    outputs = tuple(
        (lax.dynamic_slice_in_dim(entry_sum, first_row, share_rows, 1) for entry_sum in summed)
    )
    return (grad_tail, grad_head, outputs[0], outputs[1], outputs[2])


def solution(mesh):
    return jax.shard_map(
        body,
        mesh=mesh,
        in_specs=(
            P("frame", "row", None, None),
            P("row", "frame", None),
            P("frame", "row", None, None),
            P("row", "frame", None),
            P(),
            P(),
            P(),
            P(),
        ),
        out_specs=(
            P("frame", "row", None, None),
            P("row", "frame", None),
            P(None, "row", None),
            P(None, "row", None),
            P(None, "row"),
        ),
        check_vma=False,
    )
```

profile of v0, /device:TPU:1, one launch (start us, length us, event | category | flops | bytes accessed | tf_op | source)
XLA Modules:
  0.0 402.9 jit_solution(3812472840573635731)
XLA Ops:
  8.0 1.3 collective-permute-start.1
  10.0 8.8 %collective-permute-start.5 = (bf16[1,1,256]{2,1,0:T(2,128)(2,1)S(1)}, bf16[1,1,256]{2,1,0:T(2,128)(2,1)S(1)}, u32[]{:S(2)}, u32[]{:S(2)}) collective-permute-start(bf16[1,1,256]{2,1,0:T(2,128)(2,1)S(1)} %get-tuple-element.22), channel_id=1, source_target_pairs={{32,0},{64,32},{96,64},{128,96},{160,128},{192,160},{224,192},{256... | collective-permute-start | bytes 1544 | tf_op jit(solution)/shard_map/ppermute | solution.py:17
  18.8 1.9 collective-permute-start.4
  20.8 4.3 %collective-permute-start = (bf16[1,1,128,256]{3,2,1,0:T(8,128)(2,1)S(1)}, bf16[1,1,128,256]{3,2,1,0:T(8,128)(2,1)S(1)}, u32[]{:S(2)}, u32[]{:S(2)}) collective-permute-start(bf16[1,1,128,256]{3,2,1,0:T(8,128)(2,1)S(1)} %fusion.29), channel_id=1, source_target_pairs={{0,1},{1,2},{2,3},{3,4},{4,5},{5,6},{6,7},{7,8},{8,9},{9,10},{10,1... | collective-permute-start | bytes 196616 | tf_op jit(solution)/shard_map/ppermute | solution.py:16
  28.2 4.1 %all-to-all-start = ((bf16[16,2,1024]{2,1,0:T(2,128)(2,1)}), bf16[16,2,1024]{2,1,0:T(2,128)(2,1)S(1)}, u32[]{:S(2)}, u32[]{:S(2)}) async-start(bf16[16,2,1024]{2,1,0:T(2,128)(2,1)} %reshape.300), calls=%async_computation | async-start | bytes 131072 | tf_op jit(solution)/shard_map/all_to_all | solution.py:111
  32.3 1.4 collective-permute-start.7
  33.7 4.0 collective-permute-start.6
  37.7 1.3 reverse_bitcast_fusion
  44.7 7.8 %all-to-all-start.1 = ((bf16[16,1,8,256]{3,2,1,0:T(8,128)(2,1)}), bf16[16,1,8,256]{3,2,1,0:T(8,128)(2,1)S(1)}, u32[]{:S(2)}, u32[]{:S(2)}) async-start(bf16[16,1,8,256]{3,2,1,0:T(8,128)(2,1)} %slice_bitcast_fusion.45), calls=%async_computation.1 | async-start | bytes 131072 | tf_op jit(solution)/shard_map/all_to_all | solution.py:136
  53.6 2.0 collective-permute-start.9
  55.7 3.6 collective-permute-start.8
  65.9 1.3 collective-permute-start.11
  67.2 4.5 %collective-permute-start.10 = (bf16[1,10,256]{2,1,0:T(8,128)(2,1)S(1)}, bf16[1,10,256]{2,1,0:T(8,128)(2,1)S(1)}, u32[]{:S(2)}, u32[]{:S(2)}) collective-permute-start(bf16[1,10,256]{2,1,0:T(8,128)(2,1)S(1)} %pad_maximum_fusion.3), channel_id=1, source_target_pairs={{0,1},{1,2},{2,3},{3,4},{4,5},{5,6},{6,7},{7,8},{8,9},{9,10},{10,1... | collective-permute-start | bytes 15368 | tf_op jit(solution)/shard_map/ppermute | solution.py:16
  75.2 1.3 collective-permute-start.3
  76.5 5.5 %collective-permute-start.2 = (bf16[1,1,128,256]{3,2,1,0:T(8,128)(2,1)S(1)}, bf16[1,1,128,256]{3,2,1,0:T(8,128)(2,1)S(1)}, u32[]{:S(2)}, u32[]{:S(2)}) collective-permute-start(bf16[1,1,128,256]{3,2,1,0:T(8,128)(2,1)S(1)} %bitcast.414), channel_id=1, source_target_pairs={{0,1},{1,2},{2,3},{3,4},{4,5},{5,6},{6,7},{7,8},{8,9},{9,10},{10,1... | collective-permute-start | bytes 196616 | tf_op jit(solution)/shard_map/ppermute | solution.py:16
  83.9 1.4 copy-done.1
  85.5 1.0 reduce.5
  87.1 7.0 %all-to-all-start.2 = ((bf16[16,2,1024]{2,1,0:T(2,128)(2,1)}), bf16[16,2,1024]{2,1,0:T(2,128)(2,1)S(1)}, u32[]{:S(2)}, u32[]{:S(2)}) async-start(bf16[16,2,1024]{2,1,0:T(2,128)(2,1)} %reshape.302), calls=%async_computation.2 | async-start | bytes 131072 | tf_op jit(solution)/shard_map/all_to_all | solution.py:110
  94.2 4.1 %add_multiply_fusion = f32[9,256,256]{2,1,0:T(8,128)} fusion(f32[9,256,256]{2,1,0:T(8,128)} %copy-done.1, f32[9,256,256]{2,1,0:T(8,128)} %fusion.9), kind=kLoop, calls=%fused_computation | loop fusion | flops 1179648 | bytes 7077888 | tf_op jit(solution)/shard_map/mul | solution.py:153
  99.0 3.0 all-to-all-done.2
  105.8 109.8 %psum.23 = f32[2,256]{1,0:T(2,128)S(1)} all-reduce(f32[2,256]{1,0:T(2,128)S(1)} %maximum_multiply_fusion.1), channel_id=1, replica_groups=mesh['frame'=16,'row'=32] {'frame','row'}, use_global_device_ids=true, to_apply=%region_6.7 | all-reduce | flops 512 | bytes 4096 | tf_op jit(solution)/shard_map/psum | solution.py:156
  216.3 177.0 %all-reduce.9.cloned.1.call-done = (f32[9,256,256]{2,1,0:T(8,128)}, f32[3,256,256]{2,1,0:T(8,128)}) async-done(((f32[9,256,256]{2,1,0:T(8,128)}, f32[3,256,256]{2,1,0:T(8,128)}), (f32[9,256,256]{2,1,0:T(8,128)}, f32[3,256,256]{2,1,0:T(8,128)})) %all-reduce.9.cloned.1.call-update) | async-done | bytes 3145744 | tf_op jit(solution)/shard_map/psum | solution.py:156
  393.2 1.5 constant_dynamic-slice_fusion.2
  394.8 1.3 constant_dynamic-slice_fusion.1
  (134 shorter events, 29.1 us)
Async XLA Ops:
  8.0 32.3 %collective-permute-start.1 = (bf16[1,1,128,256]{3,2,1,0:T(8,128)(2,1)S(1)}, bf16[1,1,128,256]{3,2,1,0:T(8,128)(2,1)S(1)}, u32[]{:S(2)}, u32[]{:S(2)}) collective-permute-start(bf16[1,1,128,256]{3,2,1,0:T(8,128)(2,1)S(1)} %fusion.29), channel_id=1, source_target_pairs={{1,0},{2,1},{3,2},{4,3},{5,4},{6,5},{7,6},{8,7},{9,8},{10,9},{11,1... | collective-permute-start | bytes 196616 | tf_op jit(solution)/shard_map/ppermute | solution.py:17
  10.0 22.2 %collective-permute-start.5 = (bf16[1,1,256]{2,1,0:T(2,128)(2,1)S(1)}, bf16[1,1,256]{2,1,0:T(2,128)(2,1)S(1)}, u32[]{:S(2)}, u32[]{:S(2)}) collective-permute-start(bf16[1,1,256]{2,1,0:T(2,128)(2,1)S(1)} %get-tuple-element.22), channel_id=1, source_target_pairs={{32,0},{64,32},{96,64},{128,96},{160,128},{192,160},{224,192},{256... | collective-permute-start | bytes 1544 | tf_op jit(solution)/shard_map/ppermute | solution.py:17
  18.8 13.4 %collective-permute-start.4 = (bf16[1,1,256]{2,1,0:T(2,128)(2,1)S(1)}, bf16[1,1,256]{2,1,0:T(2,128)(2,1)S(1)}, u32[]{:S(2)}, u32[]{:S(2)}) collective-permute-start(bf16[1,1,256]{2,1,0:T(2,128)(2,1)S(1)} %get-tuple-element.21), channel_id=1, source_target_pairs={{0,32},{32,64},{64,96},{96,128},{128,160},{160,192},{192,224},{224... | collective-permute-start | bytes 1544 | tf_op jit(solution)/shard_map/ppermute | solution.py:16
  20.8 19.6 %collective-permute-start = (bf16[1,1,128,256]{3,2,1,0:T(8,128)(2,1)S(1)}, bf16[1,1,128,256]{3,2,1,0:T(8,128)(2,1)S(1)}, u32[]{:S(2)}, u32[]{:S(2)}) collective-permute-start(bf16[1,1,128,256]{3,2,1,0:T(8,128)(2,1)S(1)} %fusion.29), channel_id=1, source_target_pairs={{0,1},{1,2},{2,3},{3,4},{4,5},{5,6},{6,7},{7,8},{8,9},{9,10},{10,1... | collective-permute-start | bytes 196616 | tf_op jit(solution)/shard_map/ppermute | solution.py:16
  28.2 14.9 %all-to-all-start = ((bf16[16,2,1024]{2,1,0:T(2,128)(2,1)}), bf16[16,2,1024]{2,1,0:T(2,128)(2,1)S(1)}, u32[]{:S(2)}, u32[]{:S(2)}) async-start(bf16[16,2,1024]{2,1,0:T(2,128)(2,1)} %reshape.300), calls=%async_computation | async-start | bytes 131072 | tf_op jit(solution)/shard_map/all_to_all | solution.py:111
  32.3 6.8 %copy-start.8 = (bf16[1,8,256]{2,1,0:T(8,128)(2,1)S(1)}, bf16[1,8,256]{2,1,0:T(8,128)(2,1)}, u32[]{:S(2)}) copy-start(bf16[1,8,256]{2,1,0:T(8,128)(2,1)} %param.11) | copy-start | bytes 12292
  32.3 6.9 %copy-start = (bf16[9,256,256]{2,1,0:T(8,128)(2,1)S(1)}, bf16[9,256,256]{2,1,0:T(8,128)(2,1)}, u32[]{:S(2)}) copy-start(bf16[9,256,256]{2,1,0:T(8,128)(2,1)} %param.13) | copy-start | bytes 3538948
  32.3 6.8 %collective-permute-start.7 = (bf16[1,10,256]{2,1,0:T(8,128)(2,1)S(1)}, bf16[1,10,256]{2,1,0:T(8,128)(2,1)S(1)}, u32[]{:S(2)}, u32[]{:S(2)}) collective-permute-start(bf16[1,10,256]{2,1,0:T(8,128)(2,1)S(1)} %pad_maximum_fusion.2), channel_id=1, source_target_pairs={{1,0},{2,1},{3,2},{4,3},{5,4},{6,5},{7,6},{8,7},{9,8},{10,9},{11,1... | collective-permute-start | bytes 15368 | tf_op jit(solution)/shard_map/ppermute | solution.py:17
  33.7 5.4 %collective-permute-start.6 = (bf16[1,10,256]{2,1,0:T(8,128)(2,1)S(1)}, bf16[1,10,256]{2,1,0:T(8,128)(2,1)S(1)}, u32[]{:S(2)}, u32[]{:S(2)}) collective-permute-start(bf16[1,10,256]{2,1,0:T(8,128)(2,1)S(1)} %pad_maximum_fusion.2), channel_id=1, source_target_pairs={{0,1},{1,2},{2,3},{3,4},{4,5},{5,6},{6,7},{7,8},{8,9},{9,10},{10,1... | collective-permute-start | bytes 15368 | tf_op jit(solution)/shard_map/ppermute | solution.py:16
  41.3 2.1 copy-start.2
  43.1 9.4 %copy-start.10 = (f32[256]{0:T(256)S(1)}, f32[256]{0:T(256)}, u32[]{:S(2)}) copy-start(f32[256]{0:T(256)} %param.14) | copy-start | bytes 3076
  44.7 30.2 %all-to-all-start.1 = ((bf16[16,1,8,256]{3,2,1,0:T(8,128)(2,1)}), bf16[16,1,8,256]{3,2,1,0:T(8,128)(2,1)S(1)}, u32[]{:S(2)}, u32[]{:S(2)}) async-start(bf16[16,1,8,256]{3,2,1,0:T(8,128)(2,1)} %slice_bitcast_fusion.45), calls=%async_computation.1 | async-start | bytes 131072 | tf_op jit(solution)/shard_map/all_to_all | solution.py:136
  53.6 12.2 %collective-permute-start.9 = (bf16[1,1,256]{2,1,0:T(2,128)(2,1)S(1)}, bf16[1,1,256]{2,1,0:T(2,128)(2,1)S(1)}, u32[]{:S(2)}, u32[]{:S(2)}) collective-permute-start(bf16[1,1,256]{2,1,0:T(2,128)(2,1)S(1)} %get-tuple-element.20), channel_id=1, source_target_pairs={{32,0},{64,32},{96,64},{128,96},{160,128},{192,160},{224,192},{256... | collective-permute-start | bytes 1544 | tf_op jit(solution)/shard_map/ppermute | solution.py:17
  55.7 10.2 %collective-permute-start.8 = (bf16[1,1,256]{2,1,0:T(2,128)(2,1)S(1)}, bf16[1,1,256]{2,1,0:T(2,128)(2,1)S(1)}, u32[]{:S(2)}, u32[]{:S(2)}) collective-permute-start(bf16[1,1,256]{2,1,0:T(2,128)(2,1)S(1)} %get-tuple-element.19), channel_id=1, source_target_pairs={{0,32},{32,64},{64,96},{96,128},{128,160},{160,192},{192,224},{224... | collective-permute-start | bytes 1544 | tf_op jit(solution)/shard_map/ppermute | solution.py:16
  63.0 11.1 %copy-start.7 = (f32[256]{0:T(256)S(1)}, f32[256]{0:T(256)}, u32[]{:S(2)}) copy-start(f32[256]{0:T(256)} %param.12) | copy-start | bytes 3076
  63.0 11.1 %copy-start.9 = (bf16[1,8,256]{2,1,0:T(8,128)(2,1)S(1)}, bf16[1,8,256]{2,1,0:T(8,128)(2,1)}, u32[]{:S(2)}) copy-start(bf16[1,8,256]{2,1,0:T(8,128)(2,1)} %param.9) | copy-start | bytes 12292
  64.0 10.9 %copy-start.5 = (f32[128,256]{1,0:T(8,128)S(1)}, f32[128,256]{1,0:T(8,128)}, u32[]{:S(2)}) copy-start(f32[128,256]{1,0:T(8,128)} %convolution_add_fusion.10) | copy-start | bytes 393220
  64.0 10.9 %copy-start.6 = (f32[128,256]{1,0:T(8,128)S(1)}, f32[128,256]{1,0:T(8,128)}, u32[]{:S(2)}) copy-start(f32[128,256]{1,0:T(8,128)} %fusion.34) | copy-start | bytes 393220
  65.9 6.7 %collective-permute-start.11 = (bf16[1,10,256]{2,1,0:T(8,128)(2,1)S(1)}, bf16[1,10,256]{2,1,0:T(8,128)(2,1)S(1)}, u32[]{:S(2)}, u32[]{:S(2)}) collective-permute-start(bf16[1,10,256]{2,1,0:T(8,128)(2,1)S(1)} %pad_maximum_fusion.3), channel_id=1, source_target_pairs={{1,0},{2,1},{3,2},{4,3},{5,4},{6,5},{7,6},{8,7},{9,8},{10,9},{11,1... | collective-permute-start | bytes 15368 | tf_op jit(solution)/shard_map/ppermute | solution.py:17
  67.2 5.4 %collective-permute-start.10 = (bf16[1,10,256]{2,1,0:T(8,128)(2,1)S(1)}, bf16[1,10,256]{2,1,0:T(8,128)(2,1)S(1)}, u32[]{:S(2)}, u32[]{:S(2)}) collective-permute-start(bf16[1,10,256]{2,1,0:T(8,128)(2,1)S(1)} %pad_maximum_fusion.3), channel_id=1, source_target_pairs={{0,1},{1,2},{2,3},{3,4},{4,5},{5,6},{6,7},{7,8},{8,9},{9,10},{10,1... | collective-permute-start | bytes 15368 | tf_op jit(solution)/shard_map/ppermute | solution.py:16
  75.2 23.1 %collective-permute-start.3 = (bf16[1,1,128,256]{3,2,1,0:T(8,128)(2,1)S(1)}, bf16[1,1,128,256]{3,2,1,0:T(8,128)(2,1)S(1)}, u32[]{:S(2)}, u32[]{:S(2)}) collective-permute-start(bf16[1,1,128,256]{3,2,1,0:T(8,128)(2,1)S(1)} %bitcast.413), channel_id=1, source_target_pairs={{1,0},{2,1},{3,2},{4,3},{5,4},{6,5},{7,6},{8,7},{9,8},{10,9},{11,1... | collective-permute-start | bytes 196616 | tf_op jit(solution)/shard_map/ppermute | solution.py:17
  76.5 21.8 %collective-permute-start.2 = (bf16[1,1,128,256]{3,2,1,0:T(8,128)(2,1)S(1)}, bf16[1,1,128,256]{3,2,1,0:T(8,128)(2,1)S(1)}, u32[]{:S(2)}, u32[]{:S(2)}) collective-permute-start(bf16[1,1,128,256]{3,2,1,0:T(8,128)(2,1)S(1)} %bitcast.414), channel_id=1, source_target_pairs={{0,1},{1,2},{2,3},{3,4},{4,5},{5,6},{6,7},{7,8},{8,9},{9,10},{10,1... | collective-permute-start | bytes 196616 | tf_op jit(solution)/shard_map/ppermute | solution.py:16
  87.1 14.8 %all-to-all-start.2 = ((bf16[16,2,1024]{2,1,0:T(2,128)(2,1)}), bf16[16,2,1024]{2,1,0:T(2,128)(2,1)S(1)}, u32[]{:S(2)}, u32[]{:S(2)}) async-start(bf16[16,2,1024]{2,1,0:T(2,128)(2,1)} %reshape.302), calls=%async_computation.2 | async-start | bytes 131072 | tf_op jit(solution)/shard_map/all_to_all | solution.py:110
  94.1 299.1 %all-reduce.9.cloned.1.call-start = ((), (), s32[]{:S(2)}) async-start(), calls=%async_computation.3 | async-start | bytes 6291456 | tf_op jit(solution)/shard_map/psum | solution.py:156
  (3 other events, 3.5 us)
Sparse Core Ops, SparseCore 0:
  104.0 289.1 all-reduce.8
where the time goes:
time: 404 us; the launch traced here: 403 us
  waiting for transfers between devices  180 us (45%)
  blocking collectives  110 us (27%)
  starting transfers between devices  58.7 us (15%)
  matrix products  20.6 us (5%)
  between operations  14.6 us (4%)
  local copies, waits for them, and re-layouts  10.2 us (3%)
  other arithmetic  8.99 us (2%)
    psum x1, waiting for transfers between devices, body(): summed = lax.psum((kernel_sum, temporal_sum, vector_sum), ('frame', 'row'))  177 us
    psum x1, blocking collectives, body(): summed = lax.psum((kernel_sum, temporal_sum, vector_sum), ('frame', 'row'))  110 us
    ppermute x6, starting transfers between devices, padded_2(): before = lax.ppermute(last, axis, up)  23.7 us
    ppermute x6, starting transfers between devices, padded_2(): after = lax.ppermute(first, axis, down)  16.1 us
    dot_general x18, matrix products, weight_frames(): lax.dot_general(window, flattened, (((0,), (0,)), ((), ())), preferred_el...  10.4 us
    dot_general x36, matrix products, conv_frames(): jnp.dot(window, kernel[tap_index], preferred_element_type=jnp.float32)  8.91 us
  transfers between devices with their start and end apart: 16, of which 2 were waited for; matrix products, arithmetic and copies ran while one was open for 8% of the time, Pallas kernels for 0%

commit v1 on v0

v1 whole, which is shorter than its diff:
```python
import functools
import math

import jax
import jax.numpy as jnp
from jax import lax
from jax.experimental import pallas as pl
from jax.experimental.pallas import tpu as pltpu
from jax.sharding import PartitionSpec as P

MESH = pl.DeviceIdType.MESH
F32 = jnp.float32
BF16 = jnp.bfloat16
COLS = 128
CH = 256
HEAD = 8
ROWS = 160
NX, NY, NZ, NF, NR = 4, 8, 8, 16, 32
SCALE = 1.0 / math.sqrt(17 * 32 * 128)


class Slots:
    def __init__(self):
        self.count = 0

    def take(self, n):
        first = self.count
        self.count += n
        return first


S = Slots()
S_VROW, S_CNEXT, S_HV, S_CH = S.take(2), S.take(2), S.take(9), S.take(2)
S_PROW, S_PH = S.take(2), S.take(9)
S_PAIR = S.take(4)
S_X, S_Z, S_Y = S.take(9), S.take(7), S.take(7)
S_VZ, S_VX, S_VY = S.take(7), S.take(3), S.take(7)
S_CHSEND, S_VLAST = S.take(15), S.take(1)
N_SEM = S.count


def dot(a, b):
    return jnp.dot(a, b, preferred_element_type=F32)


def dot_back(a, b):
    return lax.dot_general(a, b, (((1,), (1,)), ((), ())), preferred_element_type=F32)


def dot_outer(a, b):
    return lax.dot_general(a, b, (((0,), (0,)), ((), ())), preferred_element_type=F32)


def down(v):
    return pltpu.roll(v, 1, 0)


def up(v):
    return pltpu.roll(v, v.shape[0] - 1, 0)


def kernel(
    vid_h, vh_h, cot_h, ch_h, mod_h, cw_h, cb_h, tw_h,
    gt_o, gh_o, gc_o, gtw_o, gv_o,
    vid, vh, cot, ch, mod, wv, cb, tw,
    vh32, cot32, vrow, cnext, hv, chs,
    left, lsib, right, back, prow, pgt, pgh, ph,
    prod, g, xb, h, zb, yb, total,
    vec, vzb, vxb, vyb, vpair,
    lsem, ss, rs,
):
    f = lax.axis_index("frame")
    r = lax.axis_index("row")
    y, c = lax.div(f, 2), lax.rem(f, 2)
    x, z = lax.div(r, NZ), lax.rem(r, NZ)

    def at(fo, ro):
        return (lax.rem(f + fo + NF, NF), lax.rem(r + ro + NR, NR))

    def at_x(o):
        return (f, lax.rem(x + o, NX) * NZ + z)

    def at_z(o):
        return (f, x * NZ + lax.rem(z + o, NZ))

    def at_y(o):
        return (lax.rem(y + o, NY) * 2 + c, r)

    sibling = (y * 2 + 1 - c, r)

    def remote(src, dst, send, recv, device):
        return pltpu.make_async_remote_copy(
            src_ref=src, dst_ref=dst, send_sem=ss.at[send], recv_sem=rs.at[recv],
            device_id=device, device_id_type=MESH,
        )

    pending = []

    def send(src, dst, slot, device):
        copy = remote(src, dst, slot, slot, device)
        copy.start()
        pending.append(copy)
        return copy

    pairs = [
        (vid_h, vid), (cot_h, cot), (vh_h, vh), (ch_h, ch), (mod_h, mod), (cb_h, cb),
    ] + [(cw_h.at[:, q], wv.at[q]) for q in range(3)] + [(tw_h, tw)]
    local = [pltpu.make_async_copy(a, b, lsem.at[i]) for i, (a, b) in enumerate(pairs)]
    for copy in local:
        copy.start()

    barrier = pltpu.get_barrier_semaphore()
    partners = [at(o, 0) for o in range(1, NF)]
    partners += [at_x(o) for o in range(1, NX)] + [at_z(o) for o in range(1, NZ)]
    partners += [at(fo, ro) for fo in (-1, 0, 1) for ro in (-1, 1)]
    for device in partners:
        pl.semaphore_signal(barrier, inc=1, device_id=device, device_id_type=MESH)

    for copy in local[:6]:
        copy.wait()
    vh32[...] = vh[...].astype(F32)
    cot32[...] = cot[...].astype(F32).reshape(NF, HEAD, CH)
    pl.semaphore_wait(barrier, len(partners))

    send(vid, vrow.at[0], S_VROW, at(0, 1))
    send(vid, vrow.at[1], S_VROW + 1, at(0, -1))
    around = [(dr, dc) for dr in (-1, 0, 1) for dc in (-1, 0, 1) if (dr, dc) != (0, 0)]

    def slot_of(dr, dc):
        return 3 * (dr + 1) + dc + 1

    for dr, dc in around:
        k = slot_of(dr, dc)
        send(vh32, hv.at[k], S_HV + k, at(-dc, -dr))
    send(cot, cnext.at[0], S_CNEXT, at(-1, 0))
    send(cot, cnext.at[1], S_CNEXT + 1, at(-2, 0))

    def head_cot(o):
        to = lax.rem(f + o, NF)
        return remote(cot32.at[to], chs.at[f], S_CHSEND + o - 1, S_CH + f, (to, r))

    @pl.when(f < 2)
    def _():
        for o in range(1, NF):
            head_cot(o).start()
        chs[f] = cot32[f]

    n_first = len(pending)
    for copy in pending[: n_first - 2]:
        copy.wait_recv()
    row_ids = lax.broadcasted_iota(jnp.int32, (HEAD, CH), 0)
    zero8 = jnp.zeros((HEAD, CH), F32)
    modv = mod[...]

    def row_ok(dr):
        return (r + dr >= 0) & (r + dr < NR)

    def head_block(own, pieces, dr, factor):
        ok_prev = f > 0
        ok_next = f < NF - 1
        if dr != 0:
            ok_prev = ok_prev & row_ok(dr)
            ok_next = ok_next & row_ok(dr)
        prev = jnp.where((row_ids == HEAD - 1) & ok_prev, pieces[slot_of(dr, -1)], 0.0)
        after = jnp.where((row_ids == 0) & ok_next, pieces[slot_of(dr, 1)], 0.0)
        mid = own if dr == 0 else jnp.where(row_ok(dr), pieces[slot_of(dr, 0)], 0.0)
        block = jnp.concatenate([prev, mid, after, zero8], axis=0)
        return (block * factor).astype(BF16) if factor is not None else block.astype(BF16)

    for p in range(3):
        dr = p - 1
        rows = vid[...] if dr == 0 else vrow[0 if dr < 0 else 1]
        factor = modv if dr == 0 else jnp.where(row_ok(dr), modv, 0.0)
        left[0:COLS, p * CH : (p + 1) * CH] = (rows.astype(F32) * factor).astype(BF16)
        left[COLS:ROWS, p * CH : (p + 1) * CH] = head_block(vh32[...], hv, dr, modv)

    for copy in local[6:]:
        copy.wait()

    xs = left[:, 0 : 3 * CH]
    pre = down(dot(xs, wv[0].reshape(3 * CH, CH)))
    pre = pre + dot(xs, wv[1].reshape(3 * CH, CH))
    pre = pre + up(dot(xs, wv[2].reshape(3 * CH, CH)))
    pre = pre + cb[...]
    sig = jax.nn.sigmoid(pre)
    left[:, 3 * CH : 4 * CH] = (pre * sig).astype(BF16)
    slope = sig * (1.0 + pre * (1.0 - sig))

    half_other = pl.multiple_of(2 * CH * (1 - c), 2 * CH)
    half_mine = pl.multiple_of(2 * CH * c, 2 * CH)
    send_l = send(left.at[:, pl.ds(half_other, 2 * CH)], lsib.at[1], S_PAIR, sibling)

    for copy in pending[n_first - 2 : n_first]:
        copy.wait_recv()
    for s in range(2):

        @pl.when(f != s)
        def _():
            remote(cot32.at[0], chs.at[s], S_CHSEND, S_CH + s, sibling).wait_recv()

    grad = None
    for k in range(3):
        if k == 0:
            tail, head = cot[...], ch[...].astype(F32)
        else:
            tail = jnp.where(f + k < NF, cnext[k - 1].astype(F32), 0.0).astype(BF16)
            head = chs[k - 1]
        right[1, 0, 0:COLS, k * CH : (k + 1) * CH] = tail
        right[1, 0, COLS:ROWS, k * CH : (k + 1) * CH] = jnp.concatenate(
            [zero8, head, zero8, zero8], axis=0
        ).astype(BF16)
        term = dot_back(right[1, 0, :, k * CH : (k + 1) * CH], tw[k])
        grad = term if grad is None else grad + term
    send_c = send(right.at[1, 0], right.at[1, 1], S_PAIR + 1, sibling)

    pg16 = (grad.astype(BF16).astype(F32) * slope).astype(BF16)
    pg = pg16.astype(F32)
    right[0, 0, :, 0:CH] = up(pg).astype(BF16)
    right[0, 0, :, CH : 2 * CH] = pg16
    right[0, 0, :, 2 * CH : 3 * CH] = down(pg).astype(BF16)
    send_p = send(right.at[0, 0], right.at[0, 1], S_PAIR + 2, sibling)
    pgt[...] = pg16[0:COLS]
    pgh[...] = pg[COLS + HEAD : COLS + 2 * HEAD]
    second = [send(pgt, prow.at[0], S_PROW, at(0, 1)), send(pgt, prow.at[1], S_PROW + 1, at(0, -1))]
    for dr, dc in around:
        k = slot_of(dr, dc)
        second.append(send(pgh, ph.at[k], S_PH + k, at(-dc, -dr)))
    bias_terms = jnp.sum(pg, axis=0, keepdims=True)

    lsib[0] = left[:, pl.ds(half_mine, 2 * CH)]
    send_l.wait_recv()
    send_c.wait_recv()
    send_p.wait_recv()
    xsends = {}
    for j in (1, 0):
        lhs = lsib[:, :, j * CH : (j + 1) * CH].reshape(2 * ROWS, CH)
        rhs = right[0 if j == 0 else c].reshape(2 * ROWS, 3 * CH)
        prod[j] = dot_outer(lhs, rhs)
        for t in (2,) if j == 1 else (0, 1):
            parts = [
                prod[tap // 3, :, (tap % 3) * CH : (tap % 3 + 1) * CH].reshape(NX, NZ, 8, CH)
                for tap in (2 * t, 2 * t + 1)
            ]
            g[t] = jnp.concatenate(parts, axis=2).astype(BF16)
            for o in range(1, NX):
                slot = 3 * t + o - 1
                to = lax.rem(x + o, NX)
                xsends[t, o] = send(g.at[t, to], xb.at[t, o - 1], S_X + slot, at_x(o))

    for copy in second:
        copy.wait_recv()
    for p in range(3):
        dr = 1 - p
        if dr == 0:
            rows = pgt[...]
        else:
            rows = prow[0 if dr < 0 else 1].astype(F32)
            rows = jnp.where(row_ok(dr), rows, 0.0).astype(BF16)
        back[p, 0:COLS, :] = rows
        back[p, COLS:ROWS, :] = head_block(pgh[...], ph, dr, None)
    convs = []
    for q in range(3):
        acc = None
        for p in range(3):
            term = dot_back(back[p], wv[q, p])
            acc = term if acc is None else acc + term
        convs.append(acc)
    mod_grad = up(convs[0]) + convs[1] + down(convs[2])
    tail_grad = mod_grad[0:COLS]
    head_grad = mod_grad[COLS + HEAD : COLS + 2 * HEAD]
    gt_o[...] = (cot[...].astype(F32) + modv * tail_grad).astype(BF16)
    gh_o[...] = (ch[...].astype(F32) + modv * head_grad).astype(BF16)
    scale_terms = jnp.sum(vid[...].astype(F32) * tail_grad, axis=0, keepdims=True)
    scale_terms = scale_terms + jnp.sum(vh32[...] * head_grad, axis=0, keepdims=True)
    vec[0] = jnp.concatenate(
        [
            scale_terms[:, 0:128], scale_terms[:, 128:256],
            bias_terms[:, 0:128], bias_terms[:, 128:256],
            jnp.zeros((4, 128), F32),
        ],
        axis=0,
    )
    vz = [send(vec.at[0], vzb.at[o - 1], S_VZ + o - 1, at_z(o)) for o in range(1, NZ)]

    for t in (2, 0, 1):
        acc = g[t, x].astype(F32)
        for o in range(1, NX):
            xsends[t, o].wait_recv()
            acc = acc + xb[t, o - 1].astype(F32)
        h[:, t] = acc.astype(BF16)
    zsends = []
    for o in range(1, NZ):
        zsends.append(send(h.at[lax.rem(z + o, NZ)], zb.at[o - 1], S_Z + o - 1, at_z(o)))
    acc = vec[0]
    for o in range(1, NZ):
        vz[o - 1].wait_recv()
        acc = acc + vzb[o - 1]
    vec[1] = acc
    vx = [send(vec.at[1], vxb.at[o - 1], S_VX + o - 1, at_x(o)) for o in range(1, NX)]
    acc = h[z].astype(F32)
    for o in range(1, NZ):
        zsends[o - 1].wait_recv()
        acc = acc + zb[o - 1].astype(F32)
    yb[y] = acc.astype(BF16)
    ysends = [send(yb.at[y], yb.at[y], S_Y + o - 1, at_y(o)) for o in range(1, NY)]
    acc = vec[1]
    for o in range(1, NX):
        vx[o - 1].wait_recv()
        acc = acc + vxb[o - 1]
    vyb[y] = acc
    vy = [send(vyb.at[y], vyb.at[y], S_VY + o - 1, at_y(o)) for o in range(1, NY)]
    for o in range(1, NY):
        from_y = lax.rem(y + NY - o, NY)
        remote(yb.at[from_y], yb.at[from_y], S_Y + o - 1, S_Y + o - 1, sibling).wait_recv()
        remote(vyb.at[from_y], vyb.at[from_y], S_VY + o - 1, S_VY + o - 1, sibling).wait_recv()
    acc = yb[0].astype(F32)
    vacc = vyb[0]
    for s in range(1, NY):
        acc = acc + yb[s].astype(F32)
        vacc = vacc + vyb[s]
    total[pl.ds(6 * c, 6)] = (acc * SCALE).reshape(6, 8, CH)
    vpair[0] = vacc
    mine = total.at[pl.ds(6 * c, 6)]
    theirs = total.at[pl.ds(6 * (1 - c), 6)]
    last = send(mine, mine, S_PAIR + 3, sibling)
    vlast = send(vpair.at[0], vpair.at[1], S_VLAST, sibling)
    remote(theirs, theirs, S_PAIR + 3, S_PAIR + 3, sibling).wait_recv()
    vlast.wait_recv()
    gc_o[...] = total[0:9]
    gtw_o[...] = total[9:12]
    both = (vpair[0] + vpair[1]) * SCALE
    low = r < NR // 2
    two = jnp.concatenate(
        [
            jnp.where(low, both[0:1], both[1:2]),
            jnp.where(low, both[2:3], both[3:4]),
            jnp.zeros((6, 128), F32),
        ],
        axis=0,
    )
    turned = pltpu.roll(two, lax.rem(128 - 8 * lax.rem(r, 16), 128), 1)
    gv_o[...] = turned[0:2, 0:8]

    for copy in pending:
        copy.wait_send()

    @pl.when(f < 2)
    def _():
        for o in range(1, NF):
            head_cot(o).wait_send()


def body(video_tail, video_head, cotangent_tail, cotangent_head, modulation, conv_weight, conv_bias, temporal_weight):
    any_spec = pl.BlockSpec(memory_space=pl.ANY)
    vmem = pl.BlockSpec(memory_space=pltpu.VMEM)
    scratch = [
        ((COLS, CH), BF16), ((HEAD, CH), BF16), ((COLS, CH), BF16), ((HEAD, CH), BF16),
        ((1, CH), F32), ((3, 3, CH, CH), BF16), ((1, CH), F32), ((3, CH, CH), BF16),
        ((HEAD, CH), F32), ((NF, HEAD, CH), F32), ((2, COLS, CH), BF16), ((2, COLS, CH), BF16),
        ((9, HEAD, CH), F32), ((2, HEAD, CH), F32),
        ((ROWS, 4 * CH), BF16), ((2, ROWS, 2 * CH), BF16), ((2, 2, ROWS, 3 * CH), BF16),
        ((3, ROWS, CH), BF16), ((2, COLS, CH), BF16), ((COLS, CH), BF16), ((HEAD, CH), F32),
        ((9, HEAD, CH), F32),
        ((2, CH, 3 * CH), F32), ((3, NX, NZ, 16, CH), BF16), ((3, NX - 1, NZ, 16, CH), BF16),
        ((NZ, 3, 16, CH), BF16), ((NZ - 1, 3, 16, CH), BF16), ((NY, 3, 16, CH), BF16),
        ((12, 8, CH), F32),
        ((2, 8, 128), F32), ((NZ - 1, 8, 128), F32), ((NX - 1, 8, 128), F32), ((NY, 8, 128), F32),
        ((2, 8, 128), F32),
    ]
    outs = pl.pallas_call(
        kernel,
        out_shape=(
            jax.ShapeDtypeStruct((COLS, CH), BF16),
            jax.ShapeDtypeStruct((HEAD, CH), BF16),
            jax.ShapeDtypeStruct((9, 8, CH), F32),
            jax.ShapeDtypeStruct((3, 8, CH), F32),
            jax.ShapeDtypeStruct((2, 8), F32),
        ),
        in_specs=[any_spec] * 8,
        out_specs=(vmem,) * 5,
        scratch_shapes=[pltpu.VMEM(shape, kind) for shape, kind in scratch]
        + [
            pltpu.SemaphoreType.DMA((10,)),
            pltpu.SemaphoreType.DMA((N_SEM,)),
            pltpu.SemaphoreType.DMA((N_SEM,)),
        ],
        compiler_params=pltpu.CompilerParams(
            collective_id=0, has_side_effects=True, vmem_limit_bytes=48 << 20
        ),
        name="video_block_backward",
    )(
        video_tail.reshape(COLS, CH),
        video_head.reshape(HEAD, CH),
        cotangent_tail.reshape(COLS, CH),
        cotangent_head.reshape(HEAD, CH),
        modulation.reshape(1, CH),
        conv_weight.reshape(3, 3, CH, CH),
        conv_bias.reshape(1, CH),
        temporal_weight,
    )
    return (outs[0].reshape(1, 1, COLS, CH), outs[1].reshape(1, HEAD, CH), outs[2], outs[3], outs[4])


def solution(mesh):
    return jax.shard_map(
        body,
        mesh=mesh,
        in_specs=(
            P("frame", "row", None, None),
            P("row", "frame", None),
            P("frame", "row", None, None),
            P("row", "frame", None),
            P(),
            P(),
            P(),
            P(),
        ),
        out_specs=(
            P("frame", "row", None, None),
            P("row", "frame", None),
            P(None, "row", None),
            P(None, "row", None),
            P(None, "row"),
        ),
        check_vma=False,
    )
```

time: 404 us -> 64.2 us (0.16)
  waiting for transfers between devices: 180 us -> 0 us
  blocking collectives: 110 us -> 0 us
  starting transfers between devices: 58.7 us -> 0 us
  Pallas kernels: 0 us -> 53.5 us
  matrix products: 20.6 us -> 0 us
  between operations: 14.6 us -> 0.66 us
  other arithmetic: 8.99 us -> 0 us
    psum x1 -> x0, waiting for transfers between devices: 177 us -> none  [body(): summed = lax.psum((kernel_sum, temporal_sum, vector_sum), ('frame', 'row'))]
    psum x1 -> x0, blocking collectives: 110 us -> none  [body(): summed = lax.psum((kernel_sum, temporal_sum, vector_sum), ('frame', 'row'))]
    pallas_call x0 -> x1, Pallas kernels: none -> 53.5 us  [body(): pl.pallas_call(kernel, out_shape=(jax.ShapeDtypeStruct((COLS, CH), BF16),...]
    ppermute x12 -> x0, starting transfers between devices: 39.8 us -> none  [the longest x6 23.7 us: padded_2(): before = lax.ppermute(last, axis, up)]
    dot_general x60 -> x0, matrix products: 20.6 us -> none  [the longest x18 10.4 us: weight_frames(): lax.dot_general(window, flattened, (((0,), (0,)), ((), ())), preferred_el...]
    all_to_all x3 -> x0, starting transfers between devices: 18.9 us -> none  [the longest x1 7.83 us: body(): lax.all_to_all(act_grad[1:], 'frame', split_axis=0, concat_axis=2, tiled=...]
    unnamed x33 -> x21, local copies, waits for them, and re-layouts: 4.43 us -> 9.69 us
    mul x3 -> x0, other arithmetic: 5.13 us -> none  [the longest x1 4.12 us: body(): kernel_sum = kernel_terms * norm_scale]
  transfers between devices with their start and end apart: 16 -> 0, of which waited for: 2 -> 0; matrix products, arithmetic and copies ran while one was open for 8% -> 0% of each run, Pallas kernels for 0% -> 0%
where the time goes in v1:
time: 64.2 us; the launch traced here: 63.8 us
  Pallas kernels  53.5 us (83%)
  local copies, waits for them, and re-layouts  9.69 us (15%)
  between operations  0.66 us (1%)
    pallas_call x1, Pallas kernels, body(): pl.pallas_call(kernel, out_shape=(jax.ShapeDtypeStruct((COLS, CH), BF16),...  53.5 us
    unnamed x21, local copies, waits for them, and re-layouts  9.69 us

profile of v1, /device:TPU:1, one launch (start us, length us, event | category | flops | bytes accessed | tf_op | source)
XLA Modules:
  0.0 63.8 jit_solution(9292259856307114354)
XLA Ops:
  0.6 0.0 copy-start
  0.6 1.3 %copy-done = bf16[9,256,256]{2,1,0:T(8,128)(2,1)S(1)} copy-done((bf16[9,256,256]{2,1,0:T(8,128)(2,1)S(1)}, bf16[9,256,256]{2,1,0:T(8,128)(2,1)}, u32[]{:S(2)}) %copy-start) | copy-done | bytes 1179672
  1.9 0.0 copy-start.1
  1.9 1.0 %copy-done.1 = bf16[3,256,256]{2,1,0:T(8,128)(2,1)S(1)} copy-done((bf16[3,256,256]{2,1,0:T(8,128)(2,1)S(1)}, bf16[3,256,256]{2,1,0:T(8,128)(2,1)}, u32[]{:S(2)}) %copy-start.1) | copy-done | bytes 393240
  2.9 0.0 copy-start.2
  2.9 0.8 %copy-done.2 = bf16[1,1,128,256]{3,2,1,0:T(8,128)(2,1)S(1)} copy-done((bf16[1,1,128,256]{3,2,1,0:T(8,128)(2,1)S(1)}, bf16[1,1,128,256]{3,2,1,0:T(8,128)(2,1)}, u32[]{:S(2)}) %copy-start.2) | copy-done | bytes 65560
  3.7 0.0 copy-start.3
  3.7 0.8 %copy-done.3 = bf16[1,1,128,256]{3,2,1,0:T(8,128)(2,1)S(1)} copy-done((bf16[1,1,128,256]{3,2,1,0:T(8,128)(2,1)S(1)}, bf16[1,1,128,256]{3,2,1,0:T(8,128)(2,1)}, u32[]{:S(2)}) %copy-start.3) | copy-done | bytes 65560
  4.6 0.0 copy-start.4
  4.6 0.7 %copy-done.4 = bf16[1,8,256]{2,1,0:T(8,128)(2,1)S(1)} copy-done((bf16[1,8,256]{2,1,0:T(8,128)(2,1)S(1)}, bf16[1,8,256]{2,1,0:T(8,128)(2,1)}, u32[]{:S(2)}) %copy-start.4) | copy-done | bytes 4120
  5.3 0.0 copy-start.5
  5.3 0.7 %copy-done.5 = bf16[1,8,256]{2,1,0:T(8,128)(2,1)S(1)} copy-done((bf16[1,8,256]{2,1,0:T(8,128)(2,1)S(1)}, bf16[1,8,256]{2,1,0:T(8,128)(2,1)}, u32[]{:S(2)}) %copy-start.5) | copy-done | bytes 4120
  6.0 0.0 copy-start.6
  6.0 0.7 %copy-done.6 = f32[256]{0:T(256)S(1)} copy-done((f32[256]{0:T(256)S(1)}, f32[256]{0:T(256)}, u32[]{:S(2)}) %copy-start.6) | copy-done | bytes 1048
  6.6 0.0 copy-start.7
  6.6 0.7 %copy-done.7 = f32[256]{0:T(256)S(1)} copy-done((f32[256]{0:T(256)S(1)}, f32[256]{0:T(256)}, u32[]{:S(2)}) %copy-start.7) | copy-done | bytes 1048
  7.3 53.5 %video_block_backward.1 = (bf16[128,256]{1,0:T(8,128)(2,1)S(1)}, bf16[8,256]{1,0:T(8,128)(2,1)S(1)}, f32[9,8,256]{2,1,0:T(8,128)S(1)}, f32[3,8,256]{2,1,0:T(8,128)S(1)}, f32[2,8]{1,0:T(2,128)S(1)}) custom-call(bf16[128,256]{1,0:T(8,128)(2,1)S(1)} %bitcast.11, bf16[8,256]{1,0:T(8,128)(2,1)S(1)} %bitcast.13, bf16[128,256]{1,0:T(8,128)(2,1)S(1)} %bitcast.12, ...), custom_call_target="tpu_custom_call" | custom-call | tf_op jit(solution)/shard_map/video_block_backward/pallas_call | solution.py:370
  60.8 0.6 copy.18
  61.4 0.6 copy.19
  62.0 0.6 copy.20
  62.7 0.6 copy.21
  63.3 0.6 copy.22
Async XLA Ops:
  0.6 1.3 %copy-start = (bf16[9,256,256]{2,1,0:T(8,128)(2,1)S(1)}, bf16[9,256,256]{2,1,0:T(8,128)(2,1)}, u32[]{:S(2)}) copy-start(bf16[9,256,256]{2,1,0:T(8,128)(2,1)} %param.13) | copy-start | bytes 3538948
  1.9 1.0 %copy-start.1 = (bf16[3,256,256]{2,1,0:T(8,128)(2,1)S(1)}, bf16[3,256,256]{2,1,0:T(8,128)(2,1)}, u32[]{:S(2)}) copy-start(bf16[3,256,256]{2,1,0:T(8,128)(2,1)} %tw_h.1) | copy-start | bytes 1179652
  2.9 0.8 %copy-start.2 = (bf16[1,1,128,256]{3,2,1,0:T(8,128)(2,1)S(1)}, bf16[1,1,128,256]{3,2,1,0:T(8,128)(2,1)}, u32[]{:S(2)}) copy-start(bf16[1,1,128,256]{3,2,1,0:T(8,128)(2,1)} %param.8) | copy-start | bytes 196612
  3.7 0.8 %copy-start.3 = (bf16[1,1,128,256]{3,2,1,0:T(8,128)(2,1)S(1)}, bf16[1,1,128,256]{3,2,1,0:T(8,128)(2,1)}, u32[]{:S(2)}) copy-start(bf16[1,1,128,256]{3,2,1,0:T(8,128)(2,1)} %param.10) | copy-start | bytes 196612
  4.6 0.7 %copy-start.4 = (bf16[1,8,256]{2,1,0:T(8,128)(2,1)S(1)}, bf16[1,8,256]{2,1,0:T(8,128)(2,1)}, u32[]{:S(2)}) copy-start(bf16[1,8,256]{2,1,0:T(8,128)(2,1)} %param.9) | copy-start | bytes 12292
  5.3 0.7 %copy-start.5 = (bf16[1,8,256]{2,1,0:T(8,128)(2,1)S(1)}, bf16[1,8,256]{2,1,0:T(8,128)(2,1)}, u32[]{:S(2)}) copy-start(bf16[1,8,256]{2,1,0:T(8,128)(2,1)} %param.11) | copy-start | bytes 12292
  6.0 0.7 %copy-start.6 = (f32[256]{0:T(256)S(1)}, f32[256]{0:T(256)}, u32[]{:S(2)}) copy-start(f32[256]{0:T(256)} %param.12) | copy-start | bytes 3076
  6.6 0.7 %copy-start.7 = (f32[256]{0:T(256)S(1)}, f32[256]{0:T(256)}, u32[]{:S(2)}) copy-start(f32[256]{0:T(256)} %param.14) | copy-start | bytes 3076

commit v2 on v1

v2 whole, which is shorter than its diff:
```python
import functools
import math

import jax
import jax.numpy as jnp
from jax import lax
from jax.experimental import pallas as pl
from jax.experimental.pallas import tpu as pltpu
from jax.sharding import PartitionSpec as P

MESH = pl.DeviceIdType.MESH
F32 = jnp.float32
BF16 = jnp.bfloat16
COLS = 128
CH = 256
HEAD = 8
ROWS = 160
NX, NY, NZ, NF, NR = 4, 8, 8, 16, 32
SCALE = 1.0 / math.sqrt(17 * 32 * 128)


GROUPS = (
    "vrow", "cnext", "hv", "ch0", "ch1", "prow", "ph", "lsib", "csib", "psib", "total",
    "x0", "x1", "z", "zf", "xl", "y", "vz", "vx", "vy", "vpair",
)
SEM = {name: i for i, name in enumerate(GROUPS)}


def stacked(piece):
    half = CH // 2
    return jnp.concatenate([piece[..., :half], piece[..., half:]], axis=-2).astype(BF16)


def unstacked(piece):
    rows = piece.astype(F32)
    return jnp.concatenate([rows[:HEAD], rows[HEAD:]], axis=1)


def dot(a, b):
    return jnp.dot(a, b, preferred_element_type=F32)


def dot_back(a, b):
    return lax.dot_general(a, b, (((1,), (1,)), ((), ())), preferred_element_type=F32)


def dot_outer(a, b):
    return lax.dot_general(a, b, (((0,), (0,)), ((), ())), preferred_element_type=F32)


def down(v):
    return pltpu.roll(v, 1, 0)


def up(v):
    return pltpu.roll(v, v.shape[0] - 1, 0)


def kernel(
    vid_h, vh_h, cot_h, ch_h, mod_h, cw_h, cb_h, tw_h,
    gt_o, gh_o, gc_o, gtw_o, gv_o,
    vc, heads, vecs, wv, tw, gt_v, gh_v, gc_v, gtw_v, gv_v,
    vhs, cots, vrow, cnext, hv, chs,
    left, lsib, right, back, prow, pgt, pgh, ph,
    prod, g, xb, h, zb, gz, zfb, hx, xlb, yb, total,
    vec, vzb, vxb, vyb, vpair,
    lsem, ss, rs,
):
    f = lax.axis_index("frame")
    r = lax.axis_index("row")
    y, c = lax.div(f, 2), lax.rem(f, 2)
    x, z = lax.div(r, NZ), lax.rem(r, NZ)

    def at(fo, ro):
        return (lax.rem(f + fo + NF, NF), lax.rem(r + ro + NR, NR))

    def at_x(o):
        return (f, lax.rem(x + o, NX) * NZ + z)

    def at_z(o):
        return (f, x * NZ + lax.rem(z + o, NZ))

    def at_y(o):
        return (lax.rem(y + o, NY) * 2 + c, r)

    sibling = (y * 2 + 1 - c, r)

    def remote(src, dst, sem, device):
        return pltpu.make_async_remote_copy(
            src_ref=src, dst_ref=dst, send_sem=ss.at[sem], recv_sem=rs.at[sem],
            device_id=device, device_id_type=MESH,
        )

    sent = {}

    def send(src, dst, name, device, whole):
        remote(src, dst, SEM[name], device).start()
        sent[name] = whole

    def arrived(name):
        whole = sent[name]
        remote(whole, whole, SEM[name], sibling).wait_recv()

    barrier = pltpu.get_barrier_semaphore()
    partners = [at(fo, ro) for ro in (-1, 1) for fo in (0, -1, 1)]
    partners += [at(o, 0) for o in range(1, NF)]
    partners += [at_x(o) for o in range(1, NX)] + [at_z(o) for o in range(1, NZ)]
    for device in partners:
        pl.semaphore_signal(barrier, inc=1, device_id=device, device_id_type=MESH)

    def local(group, src, dst):
        return pltpu.make_async_copy(src, dst, lsem.at[group])

    for group, src, dst in (
        (0, vid_h, vc.at[0]), (0, cot_h, vc.at[1]), (1, vh_h, heads.at[0]), (1, ch_h, heads.at[1]),
        (2, mod_h, vecs.at[0]), (2, cb_h, vecs.at[1]),
        (3, cw_h.at[:, 0], wv.at[0]), (3, cw_h.at[:, 1], wv.at[1]), (3, cw_h.at[:, 2], wv.at[2]),
        (4, tw_h, tw),
    ):
        local(group, src, dst).start()
    for group, whole in ((1, heads), (0, vc), (2, vecs)):
        local(group, whole, whole).wait()
    vid, cot = vc.at[0], vc.at[1]
    vh32, ch32 = heads[0].astype(F32), heads[1].astype(F32)
    vhs[...] = stacked(vh32)
    cots[...] = stacked(cot[...].astype(F32).reshape(NF, HEAD, CH))
    pl.semaphore_wait(barrier, len(partners))

    around = [(dr, dc) for dr in (0, -1, 1) for dc in (0, -1, 1) if (dr, dc) != (0, 0)]

    def slot_of(dr, dc):
        return (3 * dr + dc + 9) % 9 - 1

    for dr, dc in around:
        send(vhs, hv.at[slot_of(dr, dc)], "hv", at(-dc, -dr), hv)
    send(vid, vrow.at[0], "vrow", at(0, 1), vrow)
    send(vid, vrow.at[1], "vrow", at(0, -1), vrow)

    def head_cot(o):
        to = lax.rem(f + o, NF)
        return remote(cots.at[to], chs.at[f], SEM["ch0"] + f, (to, r))

    @pl.when(f < 2)
    def _():
        for o in range(1, NF):
            head_cot(o).start()
        chs[f] = cots[f]

    send(cot, cnext.at[0], "cnext", at(-1, 0), cnext)
    send(cot, cnext.at[1], "cnext", at(-2, 0), cnext)

    arrived("hv")
    arrived("vrow")
    row_ids = lax.broadcasted_iota(jnp.int32, (HEAD, CH), 0)
    zero8 = jnp.zeros((HEAD, CH), F32)
    modv = vecs[0]

    def row_ok(dr):
        return (r + dr >= 0) & (r + dr < NR)

    def head_block(own, pieces, dr, factor):
        ok_prev = f > 0
        ok_next = f < NF - 1
        if dr != 0:
            ok_prev = ok_prev & row_ok(dr)
            ok_next = ok_next & row_ok(dr)
        prev = jnp.where((row_ids == HEAD - 1) & ok_prev, unstacked(pieces[slot_of(dr, -1)]), 0.0)
        after = jnp.where((row_ids == 0) & ok_next, unstacked(pieces[slot_of(dr, 1)]), 0.0)
        mid = own if dr == 0 else jnp.where(row_ok(dr), unstacked(pieces[slot_of(dr, 0)]), 0.0)
        block = jnp.concatenate([prev, mid, after, zero8], axis=0)
        return (block * factor).astype(BF16) if factor is not None else block.astype(BF16)

    for p in range(3):
        dr = p - 1
        rows = vid[...] if dr == 0 else vrow[0 if dr < 0 else 1]
        factor = modv if dr == 0 else jnp.where(row_ok(dr), modv, 0.0)
        left[0:COLS, p * CH : (p + 1) * CH] = (rows.astype(F32) * factor).astype(BF16)
        left[COLS:ROWS, p * CH : (p + 1) * CH] = head_block(vh32, hv, dr, modv)

    local(3, wv, wv).wait()
    local(4, tw, tw).wait()

    xs = left[:, 0 : 3 * CH]
    pre = down(dot(xs, wv[0].reshape(3 * CH, CH)))
    pre = pre + dot(xs, wv[1].reshape(3 * CH, CH))
    pre = pre + up(dot(xs, wv[2].reshape(3 * CH, CH)))
    pre = pre + vecs[1]
    sig = jax.nn.sigmoid(pre)
    left[:, 3 * CH : 4 * CH] = (pre * sig).astype(BF16)
    slope = sig * (1.0 + pre * (1.0 - sig))

    half_other = pl.multiple_of(2 * CH * (1 - c), 2 * CH)
    half_mine = pl.multiple_of(2 * CH * c, 2 * CH)
    send(left.at[:, pl.ds(half_other, 2 * CH)], lsib.at[1], "lsib", sibling, lsib.at[1])

    arrived("cnext")
    for s in range(2):

        @pl.when(f != s)
        def _():
            remote(chs.at[s], chs.at[s], SEM["ch0"] + s, sibling).wait_recv()

    grad = None
    for k in range(3):
        if k == 0:
            tail, head = cot[...], ch32
        else:
            tail = jnp.where(f + k < NF, cnext[k - 1].astype(F32), 0.0).astype(BF16)
            head = unstacked(chs[k - 1])
        right[1, 0, 0:COLS, k * CH : (k + 1) * CH] = tail
        right[1, 0, COLS:ROWS, k * CH : (k + 1) * CH] = jnp.concatenate(
            [zero8, head, zero8, zero8], axis=0
        ).astype(BF16)
        term = dot_back(right[1, 0, :, k * CH : (k + 1) * CH], tw[k])
        grad = term if grad is None else grad + term
    send(right.at[1, 0], right.at[1, 1], "csib", sibling, right.at[1, 1])

    pg16 = (grad.astype(BF16).astype(F32) * slope).astype(BF16)
    pg = pg16.astype(F32)
    right[0, 0, :, CH : 2 * CH] = pg16
    theirs = right.at[0, 1, :, pl.ds(CH, CH)]
    send(right.at[0, 0, :, pl.ds(CH, CH)], theirs, "psib", sibling, theirs)
    pgt[...] = pg16[0:COLS]
    pg_head = pg[COLS + HEAD : COLS + 2 * HEAD]
    pgh[...] = stacked(pg_head)
    send(pgt, prow.at[0], "prow", at(0, 1), prow)
    send(pgt, prow.at[1], "prow", at(0, -1), prow)
    for dr, dc in around:
        send(pgh, ph.at[slot_of(dr, dc)], "ph", at(-dc, -dr), ph)
    right[0, 0, :, 0:CH] = up(pg).astype(BF16)
    right[0, 0, :, 2 * CH : 3 * CH] = down(pg).astype(BF16)
    bias_terms = jnp.sum(pg, axis=0, keepdims=True)

    lsib[0] = left[:, pl.ds(half_mine, 2 * CH)]
    arrived("lsib")
    arrived("csib")
    arrived("psib")
    other = right[0, 1, :, CH : 2 * CH].astype(F32)
    right[0, 1, :, 0:CH] = up(other).astype(BF16)
    right[0, 1, :, 2 * CH : 3 * CH] = down(other).astype(BF16)
    def pair_of_taps(t):
        parts = [
            prod[tap // 3, :, (tap % 3) * CH : (tap % 3 + 1) * CH].reshape(NX, NZ, 8, CH)
            for tap in (2 * t, 2 * t + 1)
        ]
        return jnp.concatenate(parts, axis=2).astype(BF16)

    for j in (1, 0):
        lhs = lsib[:, :, j * CH : (j + 1) * CH].reshape(2 * ROWS, CH)
        rhs = right[0 if j == 0 else c].reshape(2 * ROWS, 3 * CH)
        prod[j] = dot_outer(lhs, rhs)
        if j == 1:
            block = pair_of_taps(2)
            for i in range(NX):
                gz[:, i] = block[i]
            for o in range(1, NZ):
                to = lax.rem(z + o, NZ)
                send(gz.at[to], zfb.at[o - 1], "zf", at_z(o), zfb)
            continue
        for t in (0, 1):
            g[t] = pair_of_taps(t)
            for o in range(1, NX):
                to = lax.rem(x + o, NX)
                send(g.at[t, to], xb.at[t, o - 1], f"x{t}", at_x(o), xb.at[t])

    arrived("prow")
    arrived("ph")
    for p in range(3):
        dr = 1 - p
        if dr == 0:
            rows = pgt[...]
        else:
            rows = prow[0 if dr < 0 else 1].astype(F32)
            rows = jnp.where(row_ok(dr), rows, 0.0).astype(BF16)
        back[p, 0:COLS, :] = rows
        back[p, COLS:ROWS, :] = head_block(pg_head, ph, dr, None)
    convs = []
    for q in range(3):
        acc = None
        for p in range(3):
            term = dot_back(back[p], wv[q, p])
            acc = term if acc is None else acc + term
        convs.append(acc)
    mod_grad = up(convs[0]) + convs[1] + down(convs[2])
    tail_grad = mod_grad[0:COLS]
    head_grad = mod_grad[COLS + HEAD : COLS + 2 * HEAD]
    gt_v[...] = (cot[...].astype(F32) + modv * tail_grad).astype(BF16)
    gh_v[...] = (ch32 + modv * head_grad).astype(BF16)
    results = ((gt_v, gt_o), (gh_v, gh_o), (gc_v, gc_o), (gtw_v, gtw_o), (gv_v, gv_o))
    for i, (src, dst) in enumerate(results[:2]):
        local(i, src, dst).start()
    scale_terms = jnp.sum(vid[...].astype(F32) * tail_grad, axis=0, keepdims=True)
    scale_terms = scale_terms + jnp.sum(vh32 * head_grad, axis=0, keepdims=True)
    vec[0] = jnp.concatenate(
        [
            scale_terms[:, 0:128], scale_terms[:, 128:256],
            bias_terms[:, 0:128], bias_terms[:, 128:256],
            jnp.zeros((4, 128), F32),
        ],
        axis=0,
    )
    for o in range(1, NZ):
        send(vec.at[0], vzb.at[o - 1], "vz", at_z(o), vzb)

    def total_of(own, parts, count):
        acc = own.astype(F32)
        for i in range(count):
            acc = acc + parts[i].astype(F32)
        return acc

    for t in range(2):
        arrived(f"x{t}")
        h[:, t] = total_of(g[t, x], xb.at[t], NX - 1).astype(BF16)
    for o in range(1, NZ):
        send(h.at[lax.rem(z + o, NZ)], zb.at[o - 1], "z", at_z(o), zb)
    arrived("zf")
    hx[...] = total_of(gz[z], zfb, NZ - 1).astype(BF16)
    for o in range(1, NX):
        send(hx.at[lax.rem(x + o, NX)], xlb.at[o - 1], "xl", at_x(o), xlb)
    arrived("vz")
    vec[1] = total_of(vec[0], vzb, NZ - 1)
    for o in range(1, NX):
        send(vec.at[1], vxb.at[o - 1], "vx", at_x(o), vxb)
    arrived("xl")
    yb[y, 2] = total_of(hx[x], xlb, NX - 1).astype(BF16)
    arrived("z")
    yb[y, 0:2] = total_of(h[z], zb, NZ - 1).astype(BF16)
    for o in range(1, NY):
        send(yb.at[y], yb.at[y], "y", at_y(o), yb.at[pl.ds(0, NY - 1)])
    arrived("vx")
    vyb[y] = total_of(vec[1], vxb, NX - 1)
    for o in range(1, NY):
        send(vyb.at[y], vyb.at[y], "vy", at_y(o), vyb.at[pl.ds(0, NY - 1)])
    arrived("y")
    arrived("vy")
    acc = yb[0].astype(F32)
    vacc = vyb[0]
    for s in range(1, NY):
        acc = acc + yb[s].astype(F32)
        vacc = vacc + vyb[s]
    total[pl.ds(6 * c, 6)] = (acc * SCALE).reshape(6, 8, CH)
    vpair[0] = vacc
    mine = total.at[pl.ds(6 * c, 6)]
    send(mine, mine, "total", sibling, mine)
    send(vpair.at[0], vpair.at[1], "vpair", sibling, vpair.at[1])
    arrived("total")
    arrived("vpair")
    gc_v[...] = total[0:9]
    gtw_v[...] = total[9:12]
    both = (vpair[0] + vpair[1]) * SCALE
    low = r < NR // 2
    two = jnp.concatenate(
        [
            jnp.where(low, both[0:1], both[1:2]),
            jnp.where(low, both[2:3], both[3:4]),
            jnp.zeros((6, 128), F32),
        ],
        axis=0,
    )
    turned = pltpu.roll(two, lax.rem(128 - 8 * lax.rem(r, 16), 128), 1)
    gv_v[...] = turned[0:2, 0:8]
    for i, (src, dst) in enumerate(results[2:]):
        local(2 + i, src, dst).start()

    for name, whole in sent.items():
        remote(whole, whole, SEM[name], sibling).wait_send()

    @pl.when(f < 2)
    def _():
        whole = cots.at[pl.ds(0, NF - 1)]
        remote(whole, whole, SEM["ch0"] + f, sibling).wait_send()

    for i, (src, dst) in enumerate(results):
        local(i, src, dst).wait()


def write_out(*refs):
    sems = refs[10]
    copies = [pltpu.make_async_copy(refs[i], refs[5 + i], sems.at[i]) for i in range(5)]
    for copy in copies:
        copy.start()
    for copy in copies:
        copy.wait()


def body(video_tail, video_head, cotangent_tail, cotangent_head, modulation, conv_weight, conv_bias, temporal_weight):
    any_spec = pl.BlockSpec(memory_space=pl.ANY)
    scratch = [
        ((2, COLS, CH), BF16), ((2, HEAD, CH), BF16), ((2, 1, CH), F32),
        ((3, 3, CH, CH), BF16), ((3, CH, CH), BF16),
        ((COLS, CH), BF16), ((HEAD, CH), BF16), ((9, 8, CH), F32), ((3, 8, CH), F32), ((2, 8), F32),
        ((16, 128), BF16), ((NF, 16, 128), BF16), ((2, COLS, CH), BF16), ((2, COLS, CH), BF16),
        ((8, 16, 128), BF16), ((2, 16, 128), BF16),
        ((ROWS, 4 * CH), BF16), ((2, ROWS, 2 * CH), BF16), ((2, 2, ROWS, 3 * CH), BF16),
        ((3, ROWS, CH), BF16), ((2, COLS, CH), BF16), ((COLS, CH), BF16), ((16, 128), BF16),
        ((8, 16, 128), BF16),
        ((2, CH, 3 * CH), F32), ((2, NX, NZ, 16, CH), BF16), ((2, NX - 1, NZ, 16, CH), BF16),
        ((NZ, 2, 16, CH), BF16), ((NZ - 1, 2, 16, CH), BF16),
        ((NZ, NX, 16, CH), BF16), ((NZ - 1, NX, 16, CH), BF16), ((NX, 16, CH), BF16),
        ((NX - 1, 16, CH), BF16), ((NY, 3, 16, CH), BF16),
        ((12, 8, CH), F32),
        ((2, 8, 128), F32), ((NZ - 1, 8, 128), F32), ((NX - 1, 8, 128), F32), ((NY, 8, 128), F32),
        ((2, 8, 128), F32),
    ]
    shapes = [((COLS, CH), BF16), ((HEAD, CH), BF16), ((9, 8, CH), F32), ((3, 8, CH), F32), ((2, 8), F32)]
    operands = [
        video_tail.reshape(COLS, CH),
        video_head.reshape(HEAD, CH),
        cotangent_tail.reshape(COLS, CH),
        cotangent_head.reshape(HEAD, CH),
        modulation.reshape(1, CH),
        conv_weight.reshape(3, 3, CH, CH),
        conv_bias.reshape(1, CH),
        temporal_weight,
    ]
    outs = pl.pallas_call(
        kernel,
        out_shape=tuple(pltpu.VMEM(shape, kind) for shape, kind in shapes),
        in_specs=[any_spec] * 8,
        out_specs=(any_spec,) * 5,
        scratch_shapes=[pltpu.VMEM(shape, kind) for shape, kind in scratch]
        + [
            pltpu.SemaphoreType.DMA((5,)),
            pltpu.SemaphoreType.DMA((len(GROUPS),)),
            pltpu.SemaphoreType.DMA((len(GROUPS),)),
        ],
        compiler_params=pltpu.CompilerParams(
            collective_id=0, has_side_effects=True, vmem_limit_bytes=40 << 20
        ),
        name="video_block_backward",
    )(*[pltpu.with_memory_space_constraint(a, pltpu.HBM) for a in operands])
    outs = pl.pallas_call(
        write_out,
        out_shape=tuple(jax.ShapeDtypeStruct(shape, kind) for shape, kind in shapes),
        in_specs=[any_spec] * 5,
        out_specs=(any_spec,) * 5,
        scratch_shapes=[pltpu.SemaphoreType.DMA((5,))],
        compiler_params=pltpu.CompilerParams(vmem_limit_bytes=1 << 20),
        name="write_out",
    )(*outs)
    return (outs[0].reshape(1, 1, COLS, CH), outs[1].reshape(1, HEAD, CH), outs[2], outs[3], outs[4])


def solution(mesh):
    return jax.shard_map(
        body,
        mesh=mesh,
        in_specs=(
            P("frame", "row", None, None),
            P("row", "frame", None),
            P("frame", "row", None, None),
            P("row", "frame", None),
            P(),
            P(),
            P(),
            P(),
        ),
        out_specs=(
            P("frame", "row", None, None),
            P("row", "frame", None),
            P(None, "row", None),
            P(None, "row", None),
            P(None, "row"),
        ),
        check_vma=False,
    )
```

time: 64.2 us -> 48.8 us (0.76)
  local copies, waits for them, and re-layouts: 9.69 us -> 0 us
  Pallas kernels: 53.5 us -> 48 us
    unnamed x21 -> x0, local copies, waits for them, and re-layouts: 9.69 us -> none
    pallas_call x1 -> x2, Pallas kernels: 53.5 us -> 48 us  [the longest x1 47.3 us: body(): pl.pallas_call(kernel, out_shape=tuple((pltpu.VMEM(shape, kind) for shape...]
where the time goes in v2:
time: 48.8 us; the launch traced here: 48.7 us
  Pallas kernels  48 us (98%)
  between operations  0.64 us (1%)
    pallas_call x1, Pallas kernels, body(): pl.pallas_call(kernel, out_shape=tuple((pltpu.VMEM(shape, kind) for shape...  47.3 us

profile of v2, /device:TPU:1, one launch (start us, length us, event | category | flops | bytes accessed | tf_op | source)
XLA Modules:
  0.0 48.7 jit_solution(12048054130318572923)
XLA Ops:
  0.6 47.3 %video_block_backward.1 = (bf16[128,256]{1,0:T(8,128)(2,1)S(1)}, bf16[8,256]{1,0:T(8,128)(2,1)S(1)}, f32[9,8,256]{2,1,0:T(8,128)S(1)}, f32[3,8,256]{2,1,0:T(8,128)S(1)}, f32[2,8]{1,0:T(2,128)S(1)}) custom-call(bf16[128,256]{1,0:T(8,128)(2,1)} %bitcast.10, bf16[8,256]{1,0:T(8,128)(2,1)} %bitcast.12, bf16[128,256]{1,0:T(8,128)(2,1)} %bitcast.11, ...), custom_call_target="tpu_custom_call" | custom-call | tf_op jit(solution)/shard_map/video_block_backward/pallas_call | solution.py:416
  47.9 0.7 %write_out.1 = (bf16[128,256]{1,0:T(8,128)(2,1)}, bf16[8,256]{1,0:T(8,128)(2,1)}, f32[9,8,256]{2,1,0:T(8,128)}, f32[3,8,256]{2,1,0:T(8,128)}, f32[2,8]{1,0:T(2,128)}) custom-call(bf16[128,256]{1,0:T(8,128)(2,1)S(1)} %get-tuple-element.15.refs_0_, bf16[8,256]{1,0:T(8,128)(2,1)S(1)} %get-tuple-element.16.refs_1_, f32[9,8,256]{2,1,0:T(8,128)S(1)} %get-tuple-element.17.refs_2_, ...), custom_call_target="tpu_custom_call" | custom-call | tf_op jit(solution)/shard_map/write_out/pallas_call | solution.py:432

commit v3 on v2

v3 whole, which is shorter than its diff:
```python
import functools
import math

import jax
import jax.numpy as jnp
from jax import lax
from jax.experimental import pallas as pl
from jax.experimental.pallas import tpu as pltpu
from jax.sharding import PartitionSpec as P

MESH = pl.DeviceIdType.MESH
F32 = jnp.float32
BF16 = jnp.bfloat16
COLS = 128
CH = 256
HEAD = 8
OWN = 64
FIRST = COLS + HEAD
ROWS = 224
NX, NY, NZ, NF, NR = 4, 8, 8, 16, 32
AROUND_X = (2, 1, 3)
AROUND_8 = (4, 3, 5, 2, 6, 1, 7)
SCALE = 1.0 / math.sqrt(17 * 32 * 128)


GROUPS = (
    "vrow0", "vrow1", "cnext", "hv0", "hv1", "hv2", "hb0", "hb1", "hb2", "chg", "prow0", "prow1", "phr0", "phr1",
    "phb0", "phb1", "phb2", "gh", "lsib", "csib", "psib", "total",
    "x0", "x1", "z0", "z1", "zf", "xl", "y0", "y1", "y2", "vz", "vx", "vy",
)
SEM = {name: i for i, name in enumerate(GROUPS)}


def stacked(piece):
    half = CH // 2
    return jnp.concatenate([piece[..., :half], piece[..., half:]], axis=-2).astype(BF16)


def unstacked(piece):
    rows = piece.astype(F32)
    return jnp.concatenate([rows[:HEAD], rows[HEAD:]], axis=1)


def dot(a, b):
    return jnp.dot(a, b, preferred_element_type=F32)


def dot_back(a, b):
    return lax.dot_general(a, b, (((1,), (1,)), ((), ())), preferred_element_type=F32)


def dot_outer(a, b):
    return lax.dot_general(a, b, (((0,), (0,)), ((), ())), preferred_element_type=F32)


def down(v):
    return pltpu.roll(v, 1, 0)


def up(v):
    return pltpu.roll(v, v.shape[0] - 1, 0)


def kernel(
    vid_h, vh_h, cot_h, ch_h, mod_h, cw_h, cb_h, tw_h,
    gt_o, gh_o, taps_o, gv_o,
    vc, heads, vecs, wv, tw, gt_v, gh_v, gv_v,
    vhs, chs, vrow, cnext, hv, chg,
    left, lsib, right, back, prow, pgt, pgh, pgb, phr, phb, ghs, ghr, wsel,
    prod, g, xb, h, zb, gz, zfb, hx, xlb, yb, total,
    vec, vzb, vxb, vyb,
    lsem, ss, rs, known,
):
    f = lax.axis_index("frame")
    r = lax.axis_index("row")
    y, c = lax.div(f, 2), lax.rem(f, 2)
    x, z = lax.div(r, NZ), lax.rem(r, NZ)

    def at(fo, ro):
        return (lax.rem(f + fo + NF, NF), lax.rem(r + ro + NR, NR))

    def at_x(o):
        return (f, lax.rem(x + o, NX) * NZ + z)

    def at_z(o):
        return (f, x * NZ + lax.rem(z + o, NZ))

    def at_y(o):
        return (lax.rem(y + o, NY) * 2 + c, r)

    sibling = (y * 2 + 1 - c, r)
    low, high = f == 0, f == NF - 1
    owner = low | high
    middle = (f == NF // 2 - 1) | (f == NF // 2)
    mine_at = jnp.where(f < NF // 2, 0, NF - 1)
    place = lax.rem(f, NF // 2)

    def remote(src, dst, sem, device, recv=None):
        return pltpu.make_async_remote_copy(
            src_ref=src, dst_ref=dst, send_sem=ss.at[sem], recv_sem=rs.at[sem if recv is None else recv],
            device_id=device, device_id_type=MESH,
        )

    sent = {}

    def send(src, dst, name, device, whole):
        remote(src, dst, SEM[name], device).start()
        sent[name] = whole

    def arrived(name):
        whole = sent[name]
        remote(whole, whole, SEM[name], sibling).wait_recv()

    barrier = pltpu.get_barrier_semaphore()

    def row_ok(ro):
        return (r + ro >= 0) & (r + ro < NR)

    def greet(device, semaphore=barrier):
        pl.semaphore_signal(semaphore, inc=1, device_id=device, device_id_type=MESH)

    rows_beside = jnp.where(row_ok(-1), 1, 0) + jnp.where(row_ok(1), 1, 0)
    for ro in (-1, 1):

        @pl.when(row_ok(ro))
        def _():
            greet(at(0, ro))

    greet(sibling)
    greet(at(1, 0))
    greet(at(2, 0))
    ring = [at_x(1), at_x(NX - 1), at_z(1), at_z(NZ - 1), at_y(1), at_y(NY - 1)]
    for device in ring:
        greet(device)
    for ro in (-1, 0, 1):

        @pl.when(owner & row_ok(ro))
        def _():
            for o in range(0 if ro else 1, NF // 2 + 1):
                greet((jnp.where(low, o, NF - 1 - o), at(0, ro)[1]))
            greet((NF - 1 - f, at(0, ro)[1]))

    greeted = 9 + 2 * rows_beside + jnp.where(f != mine_at, 1, 0) + jnp.where(middle | owner, rows_beside + 1, 0)

    def local(group, src, dst):
        return pltpu.make_async_copy(src, dst, lsem.at[group])

    for group, src, dst in (
        (0, vid_h, vc.at[0]), (0, cot_h, vc.at[1]), (1, vh_h, heads.at[0]), (1, ch_h, heads.at[1]),
        (2, mod_h, vecs.at[0]), (2, cb_h, vecs.at[1]),
        (3, cw_h.at[:, 0], wv.at[0]), (3, cw_h.at[:, 1], wv.at[1]), (3, cw_h.at[:, 2], wv.at[2]),
        (4, tw_h, tw),
    ):
        local(group, src, dst).start()
    pl.semaphore_wait(barrier, greeted)
    for device in ring:
        greet(device, known.at[0])

    def head_piece(to, slot, ro, sem):
        return remote(
            vhs, hv.at[10 * (1 - ro) + slot], SEM[sem] + 1 - ro, (to, at(0, ro)[1]), SEM["hv0"] + 1 - ro
        )

    def own_piece(ro):
        return head_piece(mine_at, place + 1, ro, "hv0")

    def edge_piece(ro):
        return head_piece(NF - 1 - mine_at, jnp.where(f < NF // 2, 0, 9), ro, "hb0")

    def head_cot():
        return remote(chs, chg.at[place], SEM["chg"], (mine_at, r))

    def to_row(src, dst, name, ro):
        i = (1 - ro) // 2
        return remote(src, dst.at[i], SEM[name] + i, at(0, ro))

    def from_row(dst, name, dr):
        i = (1 + dr) // 2

        @pl.when(row_ok(dr))
        def _():
            remote(dst.at[i], dst.at[i], SEM[name] + i, sibling).wait_recv()

    for ro in (-1, 1):

        @pl.when(row_ok(ro))
        def _():
            to_row(vid_h, vrow, "vrow0", ro).start()

    send(cot_h, cnext.at[0], "cnext", at(-1, 0), cnext)
    send(cot_h, cnext.at[1], "cnext", at(-2, 0), cnext)

    for group, whole in ((1, heads), (0, vc), (2, vecs)):
        local(group, whole, whole).wait()
    vid, cot = vc.at[0], vc.at[1]
    vh32, ch32 = heads[0].astype(F32), heads[1].astype(F32)
    vhs[...] = stacked(vh32)
    chs[...] = stacked(ch32)
    left[COLS:ROWS, 0 : 3 * CH] = jnp.zeros((ROWS - COLS, 3 * CH), BF16)
    right[1, 0, COLS:ROWS, :] = jnp.zeros((ROWS - COLS, 3 * CH), BF16)
    back[:, COLS:ROWS, :] = jnp.zeros((3, ROWS - COLS, CH), BF16)
    for ro in (-1, 0, 1):

        @pl.when(row_ok(ro) if ro else f != mine_at)
        def _():
            own_piece(ro).start()

        @pl.when(middle & row_ok(ro))
        def _():
            edge_piece(ro).start()

    @pl.when(f != mine_at)
    def _():
        head_cot().start()

    @pl.when(owner)
    def _():
        hv[10 + place + 1] = vhs[...]
        chg[place] = chs[...]

    row_ids = lax.broadcasted_iota(jnp.int32, (HEAD, CH), 0)
    zero8 = jnp.zeros((HEAD, CH), F32)
    zero16 = jnp.zeros((2 * HEAD, CH), F32)
    modv = vecs[0]

    def joined(buffer, first):
        return jnp.concatenate([unstacked(buffer[first + k]) for k in range(OWN // HEAD)], axis=0)

    def head_block(before, own, after):
        before = jnp.where((row_ids == HEAD - 1) & high, unstacked(before), 0.0)
        after = jnp.where((row_ids == 0) & low, unstacked(after), 0.0)
        return jnp.concatenate([before, own, after, zero16], axis=0)

    local(4, tw, tw).wait()
    arrived("cnext")

    @pl.when(owner)
    def _():
        whole = chg.at[pl.ds(0, NF // 2 - 1)]
        remote(whole, whole, SEM["chg"], sibling).wait_recv()
        heads_of = (
            joined(chg, 0),
            jnp.where(low, cot[0:OWN].astype(F32), cnext[0, OWN:COLS].astype(F32)),
            jnp.where(low, cnext[0, 0:OWN].astype(F32), cnext[1, OWN:COLS].astype(F32)),
        )
        for k in range(3):
            block = jnp.concatenate([zero8, heads_of[k], zero8, zero16], axis=0)
            right[1, 0, COLS:ROWS, k * CH : (k + 1) * CH] = block.astype(BF16)

    grad = None
    for k in range(3):
        tail = cot[...]
        if k > 0:
            tail = jnp.where(f + k < NF, cnext[k - 1].astype(F32), 0.0).astype(BF16)
        right[1, 0, 0:COLS, k * CH : (k + 1) * CH] = tail
        term = dot_back(right[1, 0, :, k * CH : (k + 1) * CH], tw[k])
        grad = term if grad is None else grad + term
    send(right.at[1, 0], right.at[1, 1], "csib", sibling, right.at[1, 1])

    for dr in (-1, 1):
        from_row(vrow, "vrow0", dr)
    for p in range(3):
        dr = p - 1
        rows = (vid[...] if dr == 0 else vrow[0 if dr < 0 else 1]).astype(F32)
        if dr != 0:
            rows = jnp.where(row_ok(dr), rows, 0.0)
        left[0:COLS, p * CH : (p + 1) * CH] = (rows * modv).astype(BF16)

    @pl.when(owner)
    def _():
        for p in range(3):
            dr = p - 1
            pieces = hv.at[pl.ds(0, 9 if dr else 8)]

            @pl.when(row_ok(dr))
            def _():
                remote(pieces, pieces, SEM["hv0"] + p, sibling).wait_recv()

            block = head_block(hv[10 * p], joined(hv, 10 * p + 1), hv[10 * p + 9])
            if dr != 0:
                block = jnp.where(row_ok(dr), block, 0.0)
            left[COLS:ROWS, p * CH : (p + 1) * CH] = (block * modv).astype(BF16)

    pl.semaphore_wait(known.at[0], len(ring))
    further = [at_z(2), at_z(NZ - 2), at_y(2), at_y(NY - 2)]
    for device in further:
        greet(device, known.at[1])

    local(3, wv, wv).wait()

    xs = left[:, 0 : 3 * CH]
    pre = down(dot(xs, wv[0].reshape(3 * CH, CH)))
    pre = pre + dot(xs, wv[1].reshape(3 * CH, CH))
    pre = pre + up(dot(xs, wv[2].reshape(3 * CH, CH)))
    pre = pre + vecs[1]
    sig = jax.nn.sigmoid(pre)
    left[:, 3 * CH : 4 * CH] = (pre * sig).astype(BF16)
    slope = sig * (1.0 + pre * (1.0 - sig))

    half_other = pl.multiple_of(2 * CH * (1 - c), 2 * CH)
    half_mine = pl.multiple_of(2 * CH * c, 2 * CH)
    send(left.at[:, pl.ds(half_other, 2 * CH)], lsib.at[1], "lsib", sibling, lsib.at[1])

    pg16 = (grad.astype(BF16).astype(F32) * slope).astype(BF16)
    pg = pg16.astype(F32)
    right[0, 0, :, CH : 2 * CH] = pg16
    theirs = right.at[0, 1, :, pl.ds(CH, CH)]
    send(right.at[0, 0, :, pl.ds(CH, CH)], theirs, "psib", sibling, theirs)
    pgt[...] = pg16[0:COLS]
    pg_own = pg[FIRST : FIRST + OWN]
    pgh[...] = pg_own.astype(BF16)
    pgb[...] = stacked(jnp.where(low, pg_own[OWN - HEAD :], pg_own[:HEAD]))

    def head_rows(ro):
        return to_row(pgh, phr, "phr0", ro)

    def head_edge(ro):
        return remote(pgb, phb.at[1 - ro], SEM["phb0"] + 1 - ro, (NF - 1 - f, at(0, ro)[1]))

    for ro in (-1, 1):

        @pl.when(row_ok(ro))
        def _():
            to_row(pgt, prow, "prow0", ro).start()

        @pl.when(owner & row_ok(ro))
        def _():
            head_rows(ro).start()

    for ro in (-1, 0, 1):

        @pl.when(owner & row_ok(ro))
        def _():
            head_edge(ro).start()

    right[0, 0, :, 0:CH] = up(pg).astype(BF16)
    right[0, 0, :, 2 * CH : 3 * CH] = down(pg).astype(BF16)
    bias_terms = jnp.sum(pg, axis=0, keepdims=True)
    vec[0] = jnp.concatenate([bias_terms[:, 0:128], bias_terms[:, 128:256], jnp.zeros((2, 128), F32)], axis=0)

    lsib[0] = left[:, pl.ds(half_mine, 2 * CH)]

    def terms(j, core):
        return dot_outer(lsib[core, :, j * CH : (j + 1) * CH], right[0 if j == 0 else c, core])

    for j in range(2):
        prod[j] = terms(j, 0)
    arrived("lsib")
    arrived("csib")
    arrived("psib")
    other = right[0, 1, :, CH : 2 * CH].astype(F32)
    right[0, 1, :, 0:CH] = up(other).astype(BF16)
    right[0, 1, :, 2 * CH : 3 * CH] = down(other).astype(BF16)

    def pair_of_taps(t):
        parts = [
            prod[tap // 3, :, (tap % 3) * CH : (tap % 3 + 1) * CH].reshape(NX, NZ, 8, CH)
            for tap in (2 * t, 2 * t + 1)
        ]
        return jnp.concatenate(parts, axis=2).astype(BF16)

    pl.semaphore_wait(known.at[1], len(further))
    for o in AROUND_X:
        send(vec.at[0], vxb.at[o - 1], "vx", at_x(o), vxb)
    for j in range(2):
        prod[j] = prod[j] + terms(j, 1)
        for t in (0,) if j == 0 else (1,):
            g[t] = pair_of_taps(t)
            for o in AROUND_X:
                to = lax.rem(x + o, NX)
                send(g.at[t, to], xb.at[t, o - 1], f"x{t}", at_x(o), xb.at[t])
    block = pair_of_taps(2)
    for i in range(NX):
        gz[:, i] = block[i]
    for o in AROUND_8:
        send(gz.at[lax.rem(z + o, NZ)], zfb.at[o - 1], "zf", at_z(o), zfb)

    def weight_rows(tap):
        both = wv[tap % 3, tap // 3, pl.ds(pl.multiple_of(16 * lax.div(r, 2), 16), 16), :].astype(F32)
        return jnp.where(lax.rem(r, 2) == 0, both[:8], both[8:])

    for i in range(6):
        wsel[i] = jnp.where(c == 0, weight_rows(i), weight_rows(6 + i) if i < 3 else 0.0)

    for dr in (-1, 1):
        from_row(prow, "prow0", dr)
    for p in range(3):
        dr = 1 - p
        if dr == 0:
            rows = pgt[...]
        else:
            rows = prow[0 if dr < 0 else 1].astype(F32)
            rows = jnp.where(row_ok(dr), rows, 0.0).astype(BF16)
        back[p, 0:COLS, :] = rows

    @pl.when(owner)
    def _():
        for dr in (-1, 1):
            from_row(phr, "phr0", dr)
        for p in range(3):
            dr = 1 - p
            edge = phb.at[dr + 1]

            @pl.when(row_ok(dr))
            def _():
                remote(edge, edge, SEM["phb0"] + dr + 1, sibling).wait_recv()

            own = pg_own if dr == 0 else phr[0 if dr < 0 else 1].astype(F32)
            block = head_block(phb[dr + 1], own, phb[dr + 1])
            if dr != 0:
                block = jnp.where(row_ok(dr), block, 0.0)
            back[p, COLS:ROWS, :] = block.astype(BF16)

    convs = []
    for q in range(3):
        acc = None
        for p in range(3):
            term = dot_back(back[p], wv[q, p])
            acc = term if acc is None else acc + term
        convs.append(acc)
    mod_grad = up(convs[0]) + convs[1] + down(convs[2])
    tail_grad = mod_grad[0:COLS]
    head_grad = mod_grad[FIRST : FIRST + OWN]
    gt_v[...] = (cot[...].astype(F32) + modv * tail_grad).astype(BF16)

    def head_result(o):
        to = jnp.where(low, o, NF - 1 - o)
        return remote(ghs.at[lax.rem(to, NF // 2)], ghr, SEM["gh"], (to, r))

    @pl.when(owner)
    def _():
        result = joined(chg, 0) + modv * head_grad
        for k in range(OWN // HEAD):
            ghs[k] = stacked(result[k * HEAD : (k + 1) * HEAD])
        for o in range(1, NF // 2):
            head_result(o).start()
        ghr[...] = ghs[place]

    local(0, gt_v, gt_o).start()
    def total_of(own, parts, count):
        acc = own.astype(F32)
        for i in range(count):
            acc = acc + parts[i].astype(F32)
        return acc

    products = []

    def over_y(t, own):
        products.append(own[0:8] * wsel[2 * t] + own[8:16] * wsel[2 * t + 1])
        yb[y, t] = own.astype(BF16)
        for o in AROUND_8:
            send(yb.at[y, t], yb.at[y, t], f"y{t}", at_y(o), yb.at[pl.ds(0, NY - 1), t])

    arrived("vx")
    vec[1] = total_of(vec[0], vxb, NX - 1)
    for o in AROUND_8:
        send(vec.at[1], vzb.at[o - 1], "vz", at_z(o), vzb)
    for t in range(2):
        arrived(f"x{t}")
        h[t] = total_of(g[t, x], xb.at[t], NX - 1).astype(BF16)
        for o in AROUND_8:
            send(h.at[t, lax.rem(z + o, NZ)], zb.at[t, o - 1], f"z{t}", at_z(o), zb.at[t])
    arrived("zf")
    hx[...] = total_of(gz[z], zfb, NZ - 1).astype(BF16)
    for o in AROUND_X:
        send(hx.at[lax.rem(x + o, NX)], xlb.at[o - 1], "xl", at_x(o), xlb)
    arrived("z0")
    over_y(0, total_of(h[0, z], zb.at[0], NZ - 1))
    arrived("xl")
    over_y(2, total_of(hx[x], xlb, NX - 1))
    arrived("z1")
    over_y(1, total_of(h[1, z], zb.at[1], NZ - 1))
    arrived("vz")
    per_row = products[0] + products[1] + products[2]
    per_row = jnp.sum(per_row, axis=1, keepdims=True)
    lanes = lax.broadcasted_iota(jnp.int32, (8, 128), 1)
    in_lanes = jnp.where(lanes == lax.broadcasted_iota(jnp.int32, (8, 128), 0), per_row, 0.0)
    scale_terms = jnp.sum(in_lanes, axis=0, keepdims=True)
    summed = total_of(vec[1], vzb, NZ - 1)
    vyb[f] = jnp.concatenate([summed[0:2], scale_terms, jnp.zeros((1, 128), F32)], axis=0)
    for o in AROUND_8:
        for core in (c, 1 - c):
            send(vyb.at[f], vyb.at[f], "vy", (lax.rem(y + o, NY) * 2 + core, r), vyb.at[pl.ds(0, NF - 1)])
    send(vyb.at[f], vyb.at[f], "vy", sibling, vyb.at[pl.ds(0, NF - 1)])
    arrived("vy")
    both = total_of(vyb[0], vyb.at[pl.ds(1, NF - 1)], NF - 1) * SCALE
    lower = r < NR // 2
    two = jnp.concatenate(
        [
            jnp.where(lower, both[0:1], both[1:2]),
            jnp.where(lower, modv[:, 0:128], modv[:, 128:256]),
            jnp.zeros((6, 128), F32),
        ],
        axis=0,
    )
    turned = pltpu.roll(two, lax.rem(128 - 8 * lax.rem(r, 16), 128), 1)
    gv_v[...] = jnp.concatenate([both[2:3, 0:8] / turned[1:2, 0:8], turned[0:1, 0:8]], axis=0)
    local(2, gv_v, gv_o).start()

    @pl.when(f != mine_at)
    def _():
        remote(ghr, ghr, SEM["gh"], sibling).wait_recv()

    gh_v[...] = unstacked(ghr[...]).astype(BF16)
    local(1, gh_v, gh_o).start()
    for name in ("y0", "y2", "y1"):
        arrived(name)
    acc = total_of(yb[0], yb.at[pl.ds(1, NY - 1)], NY - 1)
    total[...] = (acc * SCALE).reshape(6, 8, CH)
    send(total, taps_o.at[pl.ds(6 * c, 6)], "total", sibling, total)
    local(3, total, taps_o.at[pl.ds(6 * c, 6)]).start()
    arrived("total")
    for name, whole in sent.items():
        remote(whole, whole, SEM[name], sibling).wait_send()

    for ro in (-1, 0, 1):

        @pl.when(row_ok(ro) if ro else f != mine_at)
        def _():
            own_piece(ro).wait_send()

        @pl.when(middle & row_ok(ro))
        def _():
            edge_piece(ro).wait_send()

        @pl.when(owner & row_ok(ro))
        def _():
            head_edge(ro).wait_send()
            if ro:
                head_rows(ro).wait_send()

        if ro:

            @pl.when(row_ok(ro))
            def _():
                to_row(vid, vrow, "vrow0", ro).wait_send()
                to_row(pgt, prow, "prow0", ro).wait_send()

    @pl.when(f != mine_at)
    def _():
        head_cot().wait_send()

    @pl.when(owner)
    def _():
        whole = ghs.at[pl.ds(0, NF // 2 - 1)]
        remote(whole, whole, SEM["gh"], sibling).wait_send()

    for i, whole in enumerate((gt_v, gh_v, gv_v, total)):
        local(i, whole, whole).wait()


def write_out(gt, gh, taps, gv, gt_o, gh_o, gc_o, gtw_o, gv_o, sems):
    pairs = ((gt, gt_o), (gh, gh_o), (taps.at[pl.ds(0, 9)], gc_o), (taps.at[pl.ds(9, 3)], gtw_o), (gv, gv_o))
    copies = [pltpu.make_async_copy(src, dst, sems.at[i]) for i, (src, dst) in enumerate(pairs)]
    for copy in copies:
        copy.start()
    for copy in copies:
        copy.wait()


def body(video_tail, video_head, cotangent_tail, cotangent_head, modulation, conv_weight, conv_bias, temporal_weight):
    any_spec = pl.BlockSpec(memory_space=pl.ANY)
    scratch = [
        ((2, COLS, CH), BF16), ((2, HEAD, CH), BF16), ((2, 1, CH), F32),
        ((3, 3, CH, CH), BF16), ((3, CH, CH), BF16),
        ((COLS, CH), BF16), ((HEAD, CH), BF16), ((2, 8), F32),
        ((16, 128), BF16), ((16, 128), BF16), ((2, COLS, CH), BF16), ((2, COLS, CH), BF16),
        ((30, 16, 128), BF16), ((NF // 2, 16, 128), BF16),
        ((ROWS, 4 * CH), BF16), ((2, ROWS, 2 * CH), BF16), ((2, 2, ROWS, 3 * CH), BF16),
        ((3, ROWS, CH), BF16), ((2, COLS, CH), BF16), ((COLS, CH), BF16), ((OWN, CH), BF16),
        ((16, 128), BF16), ((2, OWN, CH), BF16), ((3, 16, 128), BF16), ((NF // 2, 16, 128), BF16),
        ((16, 128), BF16), ((6, 8, CH), F32),
        ((2, CH, 3 * CH), F32), ((2, NX, NZ, 16, CH), BF16), ((2, NX - 1, NZ, 16, CH), BF16),
        ((2, NZ, 16, CH), BF16), ((2, NZ - 1, 16, CH), BF16),
        ((NZ, NX, 16, CH), BF16), ((NZ - 1, NX, 16, CH), BF16), ((NX, 16, CH), BF16),
        ((NX - 1, 16, CH), BF16), ((NY, 3, 16, CH), BF16),
        ((6, 8, CH), F32),
        ((2, 4, 128), F32), ((NZ - 1, 4, 128), F32), ((NX - 1, 4, 128), F32), ((NF, 4, 128), F32),
    ]
    shapes = [((COLS, CH), BF16), ((HEAD, CH), BF16), ((9, 8, CH), F32), ((3, 8, CH), F32), ((2, 8), F32)]
    operands = [
        video_tail.reshape(COLS, CH),
        video_head.reshape(HEAD, CH),
        cotangent_tail.reshape(COLS, CH),
        cotangent_head.reshape(HEAD, CH),
        modulation.reshape(1, CH),
        conv_weight.reshape(3, 3, CH, CH),
        conv_bias.reshape(1, CH),
        temporal_weight,
    ]
    outs = pl.pallas_call(
        kernel,
        out_shape=tuple(pltpu.VMEM(shape, kind) for shape, kind in shapes[:2] + [((12, 8, CH), F32), shapes[4]]),
        in_specs=[any_spec] * 8,
        out_specs=(any_spec,) * 4,
        scratch_shapes=[pltpu.VMEM(shape, kind) for shape, kind in scratch]
        + [
            pltpu.SemaphoreType.DMA((5,)),
            pltpu.SemaphoreType.DMA((len(GROUPS),)),
            pltpu.SemaphoreType.DMA((len(GROUPS),)),
            pltpu.SemaphoreType.REGULAR((2,)),
        ],
        compiler_params=pltpu.CompilerParams(
            collective_id=0, has_side_effects=True, vmem_limit_bytes=40 << 20
        ),
        name="video_block_backward",
    )(*[pltpu.with_memory_space_constraint(a, pltpu.HBM) for a in operands])
    outs = pl.pallas_call(
        write_out,
        out_shape=tuple(jax.ShapeDtypeStruct(shape, kind) for shape, kind in shapes),
        in_specs=[any_spec] * 4,
        out_specs=(any_spec,) * 5,
        scratch_shapes=[pltpu.SemaphoreType.DMA((5,))],
        compiler_params=pltpu.CompilerParams(vmem_limit_bytes=1 << 20),
        name="write_out",
    )(*outs)
    return (outs[0].reshape(1, 1, COLS, CH), outs[1].reshape(1, HEAD, CH), outs[2], outs[3], outs[4])


def solution(mesh):
    return jax.shard_map(
        body,
        mesh=mesh,
        in_specs=(
            P("frame", "row", None, None),
            P("row", "frame", None),
            P("frame", "row", None, None),
            P("row", "frame", None),
            P(),
            P(),
            P(),
            P(),
        ),
        out_specs=(
            P("frame", "row", None, None),
            P("row", "frame", None),
            P(None, "row", None),
            P(None, "row", None),
            P(None, "row"),
        ),
        check_vma=False,
    )
```

time: 48.8 us -> 44.7 us (0.916)
  Pallas kernels: 48 us -> 43.9 us
    pallas_call x1, Pallas kernels: 47.3 us -> 43.2 us  [body(): pl.pallas_call(kernel, out_shape=tuple((pltpu.VMEM(shape, kind) for shape...]
where the time goes in v3:
time: 44.7 us; the launch traced here: 44.6 us
  Pallas kernels  43.9 us (98%)
  between operations  0.64 us (1%)
    pallas_call x1, Pallas kernels, body(): pl.pallas_call(kernel, out_shape=tuple((pltpu.VMEM(shape, kind) for shape...  43.2 us

profile of v3, /device:TPU:1, one launch (start us, length us, event | category | flops | bytes accessed | tf_op | source)
XLA Modules:
  0.0 44.6 jit_solution(12178867854533168150)
XLA Ops:
  0.6 43.2 %video_block_backward.1 = (bf16[128,256]{1,0:T(8,128)(2,1)S(1)}, bf16[8,256]{1,0:T(8,128)(2,1)S(1)}, f32[12,8,256]{2,1,0:T(8,128)S(1)}, f32[2,8]{1,0:T(2,128)S(1)}) custom-call(bf16[128,256]{1,0:T(8,128)(2,1)} %bitcast.10, bf16[8,256]{1,0:T(8,128)(2,1)} %bitcast.12, bf16[128,256]{1,0:T(8,128)(2,1)} %bitcast.11, bf16[8,256]{1,0:T(8,128)(2,1)} %bitcast.13, ...), custom_call_target="tpu_custom_call" | custom-call | tf_op jit(solution)/shard_map/video_block_backward/pallas_call | solution.py:591
  43.9 0.7 %write_out.1 = (bf16[128,256]{1,0:T(8,128)(2,1)}, bf16[8,256]{1,0:T(8,128)(2,1)}, f32[9,8,256]{2,1,0:T(8,128)}, f32[3,8,256]{2,1,0:T(8,128)}, f32[2,8]{1,0:T(2,128)}) custom-call(bf16[128,256]{1,0:T(8,128)(2,1)S(1)} %get-tuple-element.14.gt, bf16[8,256]{1,0:T(8,128)(2,1)S(1)} %get-tuple-element.15.gh, f32[12,8,256]{2,1,0:T(8,128)S(1)} %get-tuple-element.16.taps, ...), custom_call_target="tpu_custom_call" | custom-call | tf_op jit(solution)/shard_map/write_out/pallas_call | solution.py:608

commit v4 on v3

--- a/solution.py
+++ b/solution.py
@@ -20,15 +20,18 @@
 NX, NY, NZ, NF, NR = 4, 8, 8, 16, 32
 AROUND_X = (2, 1, 3)
 AROUND_8 = (4, 3, 5, 2, 6, 1, 7)
+HALVES = (slice(0, CH // 2), slice(CH // 2, CH))
 SCALE = 1.0 / math.sqrt(17 * 32 * 128)
 
 
-GROUPS = (
-    "vrow0", "vrow1", "cnext", "hv0", "hv1", "hv2", "hb0", "hb1", "hb2", "chg", "prow0", "prow1", "phr0", "phr1",
-    "phb0", "phb1", "phb2", "gh", "lsib", "csib", "psib", "total",
-    "x0", "x1", "z0", "z1", "zf", "xl", "y0", "y1", "y2", "vz", "vx", "vy",
+ARRIVE = (
+    "vrow0", "vrow1", "cnext", "hv0", "hv1", "hv2", "chg", "prow0", "prow1", "ph0", "ph1", "ph2", "gh",
+    "sib", "psib", "total", "x0", "x1", "x2", "x3", "z0", "z1", "z2", "z3", "last1", "last2", "ends", "y", "vz", "vx", "vy",
 )
-SEM = {name: i for i, name in enumerate(GROUPS)}
+LEAVE = ("all", "up", "same", "down", "ph0", "ph1", "ph2", "vec", "odd")
+UNITS = 448
+RECV = {name: i for i, name in enumerate(ARRIVE)}
+SENT = {name: i for i, name in enumerate(LEAVE)}
 
 
 def stacked(piece):
@@ -67,9 +70,9 @@
     vc, heads, vecs, wv, tw, gt_v, gh_v, gv_v,
     vhs, chs, vrow, cnext, hv, chg,
     left, lsib, right, back, prow, pgt, pgh, pgb, phr, phb, ghs, ghr, wsel,
-    prod, g, xb, h, zb, gz, zfb, hx, xlb, yb, total,
+    prod, g, xb, h, zb, gz, zfb, hx, xlb, gy, yfb, hy, rows_in, ends, psum, yb, total,
     vec, vzb, vxb, vyb,
-    lsem, ss, rs, known,
+    sizes, lsem, ss, rs, known,
 ):
     f = lax.axis_index("frame")
     r = lax.axis_index("row")
@@ -95,21 +98,25 @@
     mine_at = jnp.where(f < NF // 2, 0, NF - 1)
     place = lax.rem(f, NF // 2)
 
-    def remote(src, dst, sem, device, recv=None):
+    def remote(src, dst, leave, arrive, device):
         return pltpu.make_async_remote_copy(
-            src_ref=src, dst_ref=dst, send_sem=ss.at[sem], recv_sem=rs.at[sem if recv is None else recv],
+            src_ref=src, dst_ref=dst, send_sem=ss.at[leave], recv_sem=rs.at[arrive],
             device_id=device, device_id_type=MESH,
         )
 
-    sent = {}
-
-    def send(src, dst, name, device, whole):
-        remote(src, dst, SEM[name], device).start()
-        sent[name] = whole
-
-    def arrived(name):
-        whole = sent[name]
-        remote(whole, whole, SEM[name], sibling).wait_recv()
+    on_both, on_0, on_1 = [], [], []
+
+    def send(src, dst, name, device, leave="all", tally=on_both):
+        remote(src, dst, SENT[leave], RECV[name], device).start()
+        if leave == "all":
+            tally.append(math.prod(src.shape) * src.dtype.itemsize // 4096)
+
+    def wait_arrived(name, whole, more=0):
+        remote(whole, whole, 0, RECV[name] + more, sibling).wait_recv()
+
+    def wait_left(name, count, more=0):
+        whole = sizes.at[pl.ds(0, count)]
+        remote(whole, whole, SENT[name] + more, 0, sibling).wait_send()
 
     barrier = pltpu.get_barrier_semaphore()
 
@@ -152,45 +159,7 @@
         (4, tw_h, tw),
     ):
         local(group, src, dst).start()
-    pl.semaphore_wait(barrier, greeted)
-    for device in ring:
-        greet(device, known.at[0])
-
-    def head_piece(to, slot, ro, sem):
-        return remote(
-            vhs, hv.at[10 * (1 - ro) + slot], SEM[sem] + 1 - ro, (to, at(0, ro)[1]), SEM["hv0"] + 1 - ro
-        )
-
-    def own_piece(ro):
-        return head_piece(mine_at, place + 1, ro, "hv0")
-
-    def edge_piece(ro):
-        return head_piece(NF - 1 - mine_at, jnp.where(f < NF // 2, 0, 9), ro, "hb0")
-
-    def head_cot():
-        return remote(chs, chg.at[place], SEM["chg"], (mine_at, r))
-
-    def to_row(src, dst, name, ro):
-        i = (1 - ro) // 2
-        return remote(src, dst.at[i], SEM[name] + i, at(0, ro))
-
-    def from_row(dst, name, dr):
-        i = (1 + dr) // 2
-
-        @pl.when(row_ok(dr))
-        def _():
-            remote(dst.at[i], dst.at[i], SEM[name] + i, sibling).wait_recv()
-
-    for ro in (-1, 1):
-
-        @pl.when(row_ok(ro))
-        def _():
-            to_row(vid_h, vrow, "vrow0", ro).start()
-
-    send(cot_h, cnext.at[0], "cnext", at(-1, 0), cnext)
-    send(cot_h, cnext.at[1], "cnext", at(-2, 0), cnext)
-
-    for group, whole in ((1, heads), (0, vc), (2, vecs)):
+    for group, whole in ((1, heads), (2, vecs), (0, vc)):
         local(group, whole, whole).wait()
     vid, cot = vc.at[0], vc.at[1]
     vh32, ch32 = heads[0].astype(F32), heads[1].astype(F32)
@@ -199,6 +168,35 @@
     left[COLS:ROWS, 0 : 3 * CH] = jnp.zeros((ROWS - COLS, 3 * CH), BF16)
     right[1, 0, COLS:ROWS, :] = jnp.zeros((ROWS - COLS, 3 * CH), BF16)
     back[:, COLS:ROWS, :] = jnp.zeros((3, ROWS - COLS, CH), BF16)
+    pl.semaphore_wait(barrier, greeted)
+    for device in ring:
+        greet(device, known.at[0])
+
+    def head_piece(to, slot, ro, leave):
+        return remote(
+            vhs, hv.at[10 * (1 - ro) + slot], SENT[leave] + 1 + ro, RECV["hv0"] + 1 - ro, (to, at(0, ro)[1])
+        )
+
+    def own_piece(ro):
+        return head_piece(mine_at, place + 1, ro, "up")
+
+    def edge_piece(ro):
+        return head_piece(NF - 1 - mine_at, jnp.where(f < NF // 2, 0, 9), ro, "ph0")
+
+    def head_cot():
+        return remote(chs, chg.at[place], SENT["same"], RECV["chg"], (mine_at, r))
+
+    def to_row(src, dst, name, ro, leave="up"):
+        i = (1 - ro) // 2
+        return remote(src, dst.at[i], SENT[leave] + 1 + ro, RECV[name] + i, at(0, ro))
+
+    def from_row(dst, name, dr):
+        i = (1 + dr) // 2
+
+        @pl.when(row_ok(dr))
+        def _():
+            wait_arrived(name, dst.at[i], i)
+
     for ro in (-1, 0, 1):
 
         @pl.when(row_ok(ro) if ro else f != mine_at)
@@ -217,6 +215,15 @@
     def _():
         hv[10 + place + 1] = vhs[...]
         chg[place] = chs[...]
+
+    for ro in (-1, 1):
+
+        @pl.when(row_ok(ro))
+        def _():
+            to_row(vid, vrow, "vrow0", ro).start()
+
+    send(cot, cnext.at[0], "cnext", at(-1, 0))
+    send(cot, cnext.at[1], "cnext", at(-2, 0))
 
     row_ids = lax.broadcasted_iota(jnp.int32, (HEAD, CH), 0)
     zero8 = jnp.zeros((HEAD, CH), F32)
@@ -232,12 +239,11 @@
         return jnp.concatenate([before, own, after, zero16], axis=0)
 
     local(4, tw, tw).wait()
-    arrived("cnext")
+    wait_arrived("cnext", cnext)
 
     @pl.when(owner)
     def _():
-        whole = chg.at[pl.ds(0, NF // 2 - 1)]
-        remote(whole, whole, SEM["chg"], sibling).wait_recv()
+        wait_arrived("chg", chg.at[pl.ds(0, NF // 2 - 1)])
         heads_of = (
             joined(chg, 0),
             jnp.where(low, cot[0:OWN].astype(F32), cnext[0, OWN:COLS].astype(F32)),
@@ -255,7 +261,12 @@
         right[1, 0, 0:COLS, k * CH : (k + 1) * CH] = tail
         term = dot_back(right[1, 0, :, k * CH : (k + 1) * CH], tw[k])
         grad = term if grad is None else grad + term
-    send(right.at[1, 0], right.at[1, 1], "csib", sibling, right.at[1, 1])
+    send(right.at[1, 0], right.at[1, 1], "sib", sibling)
+
+    pl.semaphore_wait(known.at[0], len(ring))
+    further = [at_z(2), at_z(NZ - 2), at_y(2), at_y(NY - 2)]
+    for device in further:
+        greet(device, known.at[1])
 
     for dr in (-1, 1):
         from_row(vrow, "vrow0", dr)
@@ -274,17 +285,12 @@
 
             @pl.when(row_ok(dr))
             def _():
-                remote(pieces, pieces, SEM["hv0"] + p, sibling).wait_recv()
+                wait_arrived("hv0", pieces, p)
 
             block = head_block(hv[10 * p], joined(hv, 10 * p + 1), hv[10 * p + 9])
             if dr != 0:
                 block = jnp.where(row_ok(dr), block, 0.0)
             left[COLS:ROWS, p * CH : (p + 1) * CH] = (block * modv).astype(BF16)
-
-    pl.semaphore_wait(known.at[0], len(ring))
-    further = [at_z(2), at_z(NZ - 2), at_y(2), at_y(NY - 2)]
-    for device in further:
-        greet(device, known.at[1])
 
     local(3, wv, wv).wait()
 
@@ -299,23 +305,24 @@
 
     half_other = pl.multiple_of(2 * CH * (1 - c), 2 * CH)
     half_mine = pl.multiple_of(2 * CH * c, 2 * CH)
-    send(left.at[:, pl.ds(half_other, 2 * CH)], lsib.at[1], "lsib", sibling, lsib.at[1])
+    send(left.at[:, pl.ds(half_other, 2 * CH)], lsib.at[1], "sib", sibling)
 
     pg16 = (grad.astype(BF16).astype(F32) * slope).astype(BF16)
     pg = pg16.astype(F32)
     right[0, 0, :, CH : 2 * CH] = pg16
     theirs = right.at[0, 1, :, pl.ds(CH, CH)]
-    send(right.at[0, 0, :, pl.ds(CH, CH)], theirs, "psib", sibling, theirs)
+    send(right.at[0, 0, :, pl.ds(CH, CH)], theirs, "psib", sibling)
     pgt[...] = pg16[0:COLS]
     pg_own = pg[FIRST : FIRST + OWN]
     pgh[...] = pg_own.astype(BF16)
     pgb[...] = stacked(jnp.where(low, pg_own[OWN - HEAD :], pg_own[:HEAD]))
 
     def head_rows(ro):
-        return to_row(pgh, phr, "phr0", ro)
+        i = 1 - ro
+        return remote(pgh, phr.at[i // 2], SENT["ph0"] + 1 + ro, RECV["ph0"] + i, at(0, ro))
 
     def head_edge(ro):
-        return remote(pgb, phb.at[1 - ro], SEM["phb0"] + 1 - ro, (NF - 1 - f, at(0, ro)[1]))
+        return remote(pgb, phb.at[1 - ro], SENT["ph0"] + 1 + ro, RECV["ph0"] + 1 - ro, (NF - 1 - f, at(0, ro)[1]))
 
     for ro in (-1, 1):
 
@@ -345,35 +352,64 @@
 
     for j in range(2):
         prod[j] = terms(j, 0)
-    arrived("lsib")
-    arrived("csib")
-    arrived("psib")
+    def pair_of_taps(t, lanes=slice(0, CH)):
+        parts = [
+            prod[tap // 3, :, (tap % 3) * CH + lanes.start : (tap % 3) * CH + lanes.stop].reshape(NX, NZ, 8, -1)
+            for tap in (2 * t, 2 * t + 1)
+        ]
+        return jnp.concatenate(parts, axis=2).astype(BF16)
+
+    def by_x(k, tally=on_both):
+        g[k] = pair_of_taps(k // 2, HALVES[k % 2])
+        for o in AROUND_X:
+            send(g.at[k, lax.rem(x + o, NX)], xb.at[k, o - 1], f"x{k}", at_x(o), tally=tally)
+
+    def last_products():
+        prod[1] = prod[1] + terms(1, 1)
+
+    def by_z():
+        for i in range(3):
+            block = pair_of_taps((3 + i) // 2, HALVES[(3 + i) % 2])
+            for j in range(NX):
+                gz[:, j, i] = block[j]
+        for o in AROUND_8:
+            send(gz.at[lax.rem(z + o, NZ)], zfb.at[o - 1], "last1", at_z(o), tally=on_0)
+
+    def by_y():
+        for half in range(2):
+            gy[half * NX : (half + 1) * NX] = pair_of_taps(2, HALVES[half])
+        for o in AROUND_8:
+            send(gy.at[lax.rem(y + o, NY)], yfb.at[o - 1], "last1", at_y(o), tally=on_1)
+
+    wait_arrived("sib", sizes.at[pl.ds(0, 140)])
+    pl.semaphore_wait(known.at[1], len(further))
+    for o in AROUND_X:
+        send(vec.at[0], vxb.at[o - 1], "vx", at_x(o), "vec")
+
+    @pl.when(c == 1)
+    def _():
+        last_products()
+        by_y()
+
+    wait_arrived("psib", theirs)
     other = right[0, 1, :, CH : 2 * CH].astype(F32)
     right[0, 1, :, 0:CH] = up(other).astype(BF16)
     right[0, 1, :, 2 * CH : 3 * CH] = down(other).astype(BF16)
 
-    def pair_of_taps(t):
-        parts = [
-            prod[tap // 3, :, (tap % 3) * CH : (tap % 3 + 1) * CH].reshape(NX, NZ, 8, CH)
-            for tap in (2 * t, 2 * t + 1)
-        ]
-        return jnp.concatenate(parts, axis=2).astype(BF16)
-
-    pl.semaphore_wait(known.at[1], len(further))
-    for o in AROUND_X:
-        send(vec.at[0], vxb.at[o - 1], "vx", at_x(o), vxb)
-    for j in range(2):
-        prod[j] = prod[j] + terms(j, 1)
-        for t in (0,) if j == 0 else (1,):
-            g[t] = pair_of_taps(t)
-            for o in AROUND_X:
-                to = lax.rem(x + o, NX)
-                send(g.at[t, to], xb.at[t, o - 1], f"x{t}", at_x(o), xb.at[t])
-    block = pair_of_taps(2)
-    for i in range(NX):
-        gz[:, i] = block[i]
-    for o in AROUND_8:
-        send(gz.at[lax.rem(z + o, NZ)], zfb.at[o - 1], "zf", at_z(o), zfb)
+    prod[0] = prod[0] + terms(0, 1)
+    by_x(0)
+    by_x(1)
+
+    @pl.when(c == 0)
+    def _():
+        last_products()
+        by_z()
+
+    by_x(2)
+
+    @pl.when(c == 1)
+    def _():
+        by_x(3, on_1)
 
     def weight_rows(tap):
         both = wv[tap % 3, tap // 3, pl.ds(pl.multiple_of(16 * lax.div(r, 2), 16), 16), :].astype(F32)
@@ -381,6 +417,66 @@
 
     for i in range(6):
         wsel[i] = jnp.where(c == 0, weight_rows(i), weight_rows(6 + i) if i < 3 else 0.0)
+
+    def total_of(own, parts, count):
+        acc = own.astype(F32)
+        for i in range(count):
+            acc = acc + parts[i].astype(F32)
+        return acc
+
+    psum[...] = jnp.zeros((8, 128), F32)
+
+    def over_y(k, own, tally=on_both):
+        t, lanes = k // 2, HALVES[k % 2]
+        psum[...] = psum[...] + (own[0:8] * wsel[2 * t, :, lanes] + own[8:16] * wsel[2 * t + 1, :, lanes])
+        yb[y, k] = own.astype(BF16)
+        for o in AROUND_8:
+            send(yb.at[y, k], yb.at[y, k], "y", at_y(o), tally=tally)
+
+    def vec_left(whole):
+        remote(whole, whole, SENT["vec"], 0, sibling).wait_send()
+
+    wait_arrived("vx", vxb)
+    vec_left(vxb)
+    vec[1] = total_of(vec[0], vxb, NX - 1)
+    for o in AROUND_8:
+        send(vec.at[1], vzb.at[o - 1], "vz", at_z(o), "vec")
+
+    def x_to_z(k, tally=on_both):
+        wait_arrived(f"x{k}", xb.at[k])
+        h[k] = total_of(g[k, x], xb.at[k], NX - 1).astype(BF16)
+        for o in AROUND_8:
+            send(h.at[k, lax.rem(z + o, NZ)], zb.at[k, o - 1], f"z{k}", at_z(o), tally=tally)
+
+    for k in range(3):
+        x_to_z(k)
+
+    belongs = lax.rem(y, NX)
+
+    def to_its_row(i):
+        return remote(hy.at[i], rows_in.at[r], SENT["odd"], RECV["last2"], (f, belongs * NZ + i))
+
+    @pl.when(c == 0)
+    def _():
+        wait_arrived("last1", zfb)
+        hx[...] = total_of(gz[z], zfb, NZ - 1).astype(BF16)
+        for o in AROUND_X:
+            send(hx.at[lax.rem(x + o, NX)], xlb.at[o - 1], "last2", at_x(o), tally=on_0)
+
+    @pl.when(c == 1)
+    def _():
+        x_to_z(3, on_1)
+        wait_arrived("last1", yfb)
+        hy[...] = total_of(gy[y], yfb, NY - 1).astype(BF16)
+        for i in range(NZ):
+
+            @pl.when((x != belongs) | (z != i))
+            def _():
+                to_its_row(i).start()
+
+        @pl.when(x == belongs)
+        def _():
+            rows_in[r] = hy[z]
 
     for dr in (-1, 1):
         from_row(prow, "prow0", dr)
@@ -395,15 +491,11 @@
 
     @pl.when(owner)
     def _():
-        for dr in (-1, 1):
-            from_row(phr, "phr0", dr)
         for p in range(3):
             dr = 1 - p
-            edge = phb.at[dr + 1]
-
             @pl.when(row_ok(dr))
             def _():
-                remote(edge, edge, SEM["phb0"] + dr + 1, sibling).wait_recv()
+                wait_arrived("ph0", sizes.at[pl.ds(0, 9 if dr else 1)], dr + 1)
 
             own = pg_own if dr == 0 else phr[0 if dr < 0 else 1].astype(F32)
             block = head_block(phb[dr + 1], own, phb[dr + 1])
@@ -425,7 +517,7 @@
 
     def head_result(o):
         to = jnp.where(low, o, NF - 1 - o)
-        return remote(ghs.at[lax.rem(to, NF // 2)], ghr, SEM["gh"], (to, r))
+        return remote(ghs.at[lax.rem(to, NF // 2)], ghr, SENT["ph1"], RECV["gh"], (to, r))
 
     @pl.when(owner)
     def _():
@@ -437,41 +529,33 @@
         ghr[...] = ghs[place]
 
     local(0, gt_v, gt_o).start()
-    def total_of(own, parts, count):
-        acc = own.astype(F32)
-        for i in range(count):
-            acc = acc + parts[i].astype(F32)
-        return acc
-
-    products = []
-
-    def over_y(t, own):
-        products.append(own[0:8] * wsel[2 * t] + own[8:16] * wsel[2 * t + 1])
-        yb[y, t] = own.astype(BF16)
-        for o in AROUND_8:
-            send(yb.at[y, t], yb.at[y, t], f"y{t}", at_y(o), yb.at[pl.ds(0, NY - 1), t])
-
-    arrived("vx")
-    vec[1] = total_of(vec[0], vxb, NX - 1)
-    for o in AROUND_8:
-        send(vec.at[1], vzb.at[o - 1], "vz", at_z(o), vzb)
-    for t in range(2):
-        arrived(f"x{t}")
-        h[t] = total_of(g[t, x], xb.at[t], NX - 1).astype(BF16)
-        for o in AROUND_8:
-            send(h.at[t, lax.rem(z + o, NZ)], zb.at[t, o - 1], f"z{t}", at_z(o), zb.at[t])
-    arrived("zf")
-    hx[...] = total_of(gz[z], zfb, NZ - 1).astype(BF16)
-    for o in AROUND_X:
-        send(hx.at[lax.rem(x + o, NX)], xlb.at[o - 1], "xl", at_x(o), xlb)
-    arrived("z0")
-    over_y(0, total_of(h[0, z], zb.at[0], NZ - 1))
-    arrived("xl")
-    over_y(2, total_of(hx[x], xlb, NX - 1))
-    arrived("z1")
-    over_y(1, total_of(h[1, z], zb.at[1], NZ - 1))
-    arrived("vz")
-    per_row = products[0] + products[1] + products[2]
+
+    def z_to_y(k, tally=on_both):
+        wait_arrived(f"z{k}", zb.at[k])
+        over_y(k, total_of(h[k, z], zb.at[k], NZ - 1), tally)
+
+    def to_all(o):
+        half = lax.div(y, NX)
+        return remote(ends.at[half], ends.at[half], SENT["odd"], RECV["ends"], at_y(o))
+
+    z_to_y(0)
+    z_to_y(1)
+    z_to_y(2)
+
+    @pl.when(c == 1)
+    def _():
+        z_to_y(3, on_1)
+
+    @pl.when(c == 0)
+    def _():
+        wait_arrived("last2", xlb)
+        acc = total_of(hx[x], xlb, NX - 1)
+        for i in range(3):
+            over_y(3 + i, acc[i], on_0)
+
+    wait_arrived("vz", vzb)
+    vec_left(vzb)
+    per_row = psum[...]
     per_row = jnp.sum(per_row, axis=1, keepdims=True)
     lanes = lax.broadcasted_iota(jnp.int32, (8, 128), 1)
     in_lanes = jnp.where(lanes == lax.broadcasted_iota(jnp.int32, (8, 128), 0), per_row, 0.0)
@@ -480,9 +564,23 @@
     vyb[f] = jnp.concatenate([summed[0:2], scale_terms, jnp.zeros((1, 128), F32)], axis=0)
     for o in AROUND_8:
         for core in (c, 1 - c):
-            send(vyb.at[f], vyb.at[f], "vy", (lax.rem(y + o, NY) * 2 + core, r), vyb.at[pl.ds(0, NF - 1)])
-    send(vyb.at[f], vyb.at[f], "vy", sibling, vyb.at[pl.ds(0, NF - 1)])
-    arrived("vy")
+            send(vyb.at[f], vyb.at[f], "vy", (lax.rem(y + o, NY) * 2 + core, r), "vec")
+    send(vyb.at[f], vyb.at[f], "vy", sibling, "vec")
+    @pl.when(c == 1)
+    def _():
+        @pl.when(x != belongs)
+        def _():
+            wait_left("odd", NZ)
+
+        @pl.when(x == belongs)
+        def _():
+            wait_left("odd", NZ - 1)
+            wait_arrived("last2", rows_in.at[pl.ds(0, NR - 1)])
+            ends[lax.div(y, NX)] = total_of(rows_in[0], rows_in.at[pl.ds(1, NR - 1)], NR - 1)
+            for o in AROUND_8:
+                to_all(o).start()
+
+    wait_arrived("vy", vyb.at[pl.ds(0, NF - 1)])
     both = total_of(vyb[0], vyb.at[pl.ds(1, NF - 1)], NF - 1) * SCALE
     lower = r < NR // 2
     two = jnp.concatenate(
@@ -499,51 +597,59 @@
 
     @pl.when(f != mine_at)
     def _():
-        remote(ghr, ghr, SEM["gh"], sibling).wait_recv()
+        wait_arrived("gh", ghr)
 
     gh_v[...] = unstacked(ghr[...]).astype(BF16)
     local(1, gh_v, gh_o).start()
-    for name in ("y0", "y2", "y1"):
-        arrived(name)
+
+    @pl.when(c == 0)
+    def _():
+        wait_arrived("y", yb.at[pl.ds(0, NY - 1)])
+
+    @pl.when(c == 1)
+    def _():
+        wait_arrived("y", yb.at[pl.ds(0, NY - 1), pl.ds(0, 4)])
+
+        @pl.when(x == belongs)
+        def _():
+            wait_arrived("ends", ends.at[0])
+            wait_left("odd", 2 * (NY - 1))
+
+        @pl.when(x != belongs)
+        def _():
+            wait_arrived("ends", ends)
+
     acc = total_of(yb[0], yb.at[pl.ds(1, NY - 1)], NY - 1)
-    total[...] = (acc * SCALE).reshape(6, 8, CH)
-    send(total, taps_o.at[pl.ds(6 * c, 6)], "total", sibling, total)
+    for t in range(3):
+        both = jnp.concatenate([acc[2 * t], acc[2 * t + 1]], axis=1)
+        if t == 2:
+            both = jnp.where(c == 0, both, jnp.concatenate([ends[0], ends[1]], axis=1))
+        total[2 * t : 2 * t + 2] = (both * SCALE).reshape(2, 8, CH)
+    send(total, taps_o.at[pl.ds(6 * c, 6)], "total", sibling)
     local(3, total, taps_o.at[pl.ds(6 * c, 6)]).start()
-    arrived("total")
-    for name, whole in sent.items():
-        remote(whole, whole, SEM[name], sibling).wait_send()
-
+    wait_arrived("total", total)
+
+    @pl.when(c == 0)
+    def _():
+        wait_left("all", sum(on_both) + sum(on_0))
+
+    @pl.when(c == 1)
+    def _():
+        wait_left("all", sum(on_both) + sum(on_1))
+
+    vec_left(vyb.at[pl.ds(0, NF - 1)])
     for ro in (-1, 0, 1):
-
         @pl.when(row_ok(ro) if ro else f != mine_at)
         def _():
-            own_piece(ro).wait_send()
+            wait_left("up", 33 if ro else 2, 1 + ro)
 
         @pl.when(middle & row_ok(ro))
         def _():
-            edge_piece(ro).wait_send()
+            wait_left("ph0", 1, 1 + ro)
 
         @pl.when(owner & row_ok(ro))
         def _():
-            head_edge(ro).wait_send()
-            if ro:
-                head_rows(ro).wait_send()
-
-        if ro:
-
-            @pl.when(row_ok(ro))
-            def _():
-                to_row(vid, vrow, "vrow0", ro).wait_send()
-                to_row(pgt, prow, "prow0", ro).wait_send()
-
-    @pl.when(f != mine_at)
-    def _():
-        head_cot().wait_send()
-
-    @pl.when(owner)
-    def _():
-        whole = ghs.at[pl.ds(0, NF // 2 - 1)]
-        remote(whole, whole, SEM["gh"], sibling).wait_send()
+            wait_left("ph0", 9 if ro else NF // 2, 1 + ro)
 
     for i, whole in enumerate((gt_v, gh_v, gv_v, total)):
         local(i, whole, whole).wait()
@@ -570,12 +676,15 @@
         ((3, ROWS, CH), BF16), ((2, COLS, CH), BF16), ((COLS, CH), BF16), ((OWN, CH), BF16),
         ((16, 128), BF16), ((2, OWN, CH), BF16), ((3, 16, 128), BF16), ((NF // 2, 16, 128), BF16),
         ((16, 128), BF16), ((6, 8, CH), F32),
-        ((2, CH, 3 * CH), F32), ((2, NX, NZ, 16, CH), BF16), ((2, NX - 1, NZ, 16, CH), BF16),
-        ((2, NZ, 16, CH), BF16), ((2, NZ - 1, 16, CH), BF16),
-        ((NZ, NX, 16, CH), BF16), ((NZ - 1, NX, 16, CH), BF16), ((NX, 16, CH), BF16),
-        ((NX - 1, 16, CH), BF16), ((NY, 3, 16, CH), BF16),
+        ((2, CH, 3 * CH), F32), ((4, NX, NZ, 16, 128), BF16), ((4, NX - 1, NZ, 16, 128), BF16),
+        ((4, NZ, 16, 128), BF16), ((4, NZ - 1, 16, 128), BF16),
+        ((NZ, NX, 3, 16, 128), BF16), ((NZ - 1, NX, 3, 16, 128), BF16), ((NX, 3, 16, 128), BF16),
+        ((NX - 1, 3, 16, 128), BF16),
+        ((NY, NZ, 16, 128), BF16), ((NY - 1, NZ, 16, 128), BF16), ((NZ, 16, 128), BF16), ((NR, 16, 128), BF16),
+        ((2, 16, 128), F32), ((8, 128), F32), ((NY, 6, 16, 128), BF16),
         ((6, 8, CH), F32),
         ((2, 4, 128), F32), ((NZ - 1, 4, 128), F32), ((NX - 1, 4, 128), F32), ((NF, 4, 128), F32),
+        ((UNITS, 8, 128), F32),
     ]
     shapes = [((COLS, CH), BF16), ((HEAD, CH), BF16), ((9, 8, CH), F32), ((3, 8, CH), F32), ((2, 8), F32)]
     operands = [
@@ -596,8 +705,8 @@
         scratch_shapes=[pltpu.VMEM(shape, kind) for shape, kind in scratch]
         + [
             pltpu.SemaphoreType.DMA((5,)),
-            pltpu.SemaphoreType.DMA((len(GROUPS),)),
-            pltpu.SemaphoreType.DMA((len(GROUPS),)),
+            pltpu.SemaphoreType.DMA((len(LEAVE),)),
+            pltpu.SemaphoreType.DMA((len(ARRIVE),)),
             pltpu.SemaphoreType.REGULAR((2,)),
         ],
         compiler_params=pltpu.CompilerParams(

time: 44.7 us -> 43.1 us (0.964)
  Pallas kernels: 43.9 us -> 42.3 us
    pallas_call x1, Pallas kernels: 43.2 us -> 41.6 us  [body(): pl.pallas_call(kernel, out_shape=tuple((pltpu.VMEM(shape, kind) for shape...]
where the time goes in v4:
time: 43.1 us; the launch traced here: 43 us
  Pallas kernels  42.3 us (98%)
  between operations  0.64 us (1%)
    pallas_call x1, Pallas kernels, body(): pl.pallas_call(kernel, out_shape=tuple((pltpu.VMEM(shape, kind) for shape...  41.6 us

profile of v4, /device:TPU:1, one launch (start us, length us, event | category | flops | bytes accessed | tf_op | source)
XLA Modules:
  0.0 43.0 jit_solution(9262102917213452342)
XLA Ops:
  0.6 41.6 %video_block_backward.1 = (bf16[128,256]{1,0:T(8,128)(2,1)S(1)}, bf16[8,256]{1,0:T(8,128)(2,1)S(1)}, f32[12,8,256]{2,1,0:T(8,128)S(1)}, f32[2,8]{1,0:T(2,128)S(1)}) custom-call(bf16[128,256]{1,0:T(8,128)(2,1)} %bitcast.10, bf16[8,256]{1,0:T(8,128)(2,1)} %bitcast.12, bf16[128,256]{1,0:T(8,128)(2,1)} %bitcast.11, bf16[8,256]{1,0:T(8,128)(2,1)} %bitcast.13, ...), custom_call_target="tpu_custom_call" | custom-call | tf_op jit(solution)/shard_map/video_block_backward/pallas_call | solution.py:700
  42.3 0.7 %write_out.1 = (bf16[128,256]{1,0:T(8,128)(2,1)}, bf16[8,256]{1,0:T(8,128)(2,1)}, f32[9,8,256]{2,1,0:T(8,128)}, f32[3,8,256]{2,1,0:T(8,128)}, f32[2,8]{1,0:T(2,128)}) custom-call(bf16[128,256]{1,0:T(8,128)(2,1)S(1)} %get-tuple-element.14.gt, bf16[8,256]{1,0:T(8,128)(2,1)S(1)} %get-tuple-element.15.gh, f32[12,8,256]{2,1,0:T(8,128)S(1)} %get-tuple-element.16.taps, ...), custom_call_target="tpu_custom_call" | custom-call | tf_op jit(solution)/shard_map/write_out/pallas_call | solution.py:717

commit v5 on v4

--- a/solution.py
+++ b/solution.py
@@ -26,9 +26,10 @@
 
 ARRIVE = (
     "vrow0", "vrow1", "cnext", "hv0", "hv1", "hv2", "chg", "prow0", "prow1", "ph0", "ph1", "ph2", "gh",
-    "sib", "psib", "total", "x0", "x1", "x2", "x3", "z0", "z1", "z2", "z3", "last1", "last2", "ends", "y", "vz", "vx", "vy",
+    "sib", "psib", "total", "x0", "x1", "x2", "x3", "z0", "z1", "z2", "z3", "last1", "last2", "ends", "late1", "late2", "late3", "y", "vz", "vx", "vy",
 )
-LEAVE = ("all", "up", "same", "down", "ph0", "ph1", "ph2", "vec", "odd")
+LEAVE = ("all", "up", "same", "down", "ph0", "ph1", "ph2", "vec", "odd", "late")
+OVER_Y = (("late1", "late2", "late3", "late"), ("last1", "last2", "ends", "odd"))
 UNITS = 448
 RECV = {name: i for i, name in enumerate(ARRIVE)}
 SENT = {name: i for i, name in enumerate(LEAVE)}
@@ -56,12 +57,18 @@
     return lax.dot_general(a, b, (((0,), (0,)), ((), ())), preferred_element_type=F32)
 
 
+def edge_cleared(v, row):
+    if v.shape[0] != COLS:
+        return v
+    return jnp.where(lax.broadcasted_iota(jnp.int32, v.shape, 0) == row, 0.0, v)
+
+
 def down(v):
-    return pltpu.roll(v, 1, 0)
+    return edge_cleared(pltpu.roll(v, 1, 0), 0)
 
 
 def up(v):
-    return pltpu.roll(v, v.shape[0] - 1, 0)
+    return edge_cleared(pltpu.roll(v, v.shape[0] - 1, 0), COLS - 1)
 
 
 def kernel(
@@ -70,7 +77,7 @@
     vc, heads, vecs, wv, tw, gt_v, gh_v, gv_v,
     vhs, chs, vrow, cnext, hv, chg,
     left, lsib, right, back, prow, pgt, pgh, pgb, phr, phb, ghs, ghr, wsel,
-    prod, g, xb, h, zb, gz, zfb, hx, xlb, gy, yfb, hy, rows_in, ends, psum, yb, total,
+    grads, prod, g, xb, h, zb, gz, zfb, hx, xlb, gy, yfb, hy, rows_in, ends, psum, yb, total,
     vec, vzb, vxb, vyb,
     sizes, lsem, ss, rs, known,
 ):
@@ -94,6 +101,7 @@
     sibling = (y * 2 + 1 - c, r)
     low, high = f == 0, f == NF - 1
     owner = low | high
+    with_head = (y == 0) | (y == NY - 1)
     middle = (f == NF // 2 - 1) | (f == NF // 2)
     mine_at = jnp.where(f < NF // 2, 0, NF - 1)
     place = lax.rem(f, NF // 2)
@@ -105,6 +113,12 @@
         )
 
     on_both, on_0, on_1 = [], [], []
+    on_rows = {ROWS: [], COLS: []}
+
+    def by_rows(part):
+        for rows, here in ((ROWS, with_head), (COLS, jnp.logical_not(with_head))):
+            pl.when(here)(functools.partial(part, rows))
+
 
     def send(src, dst, name, device, leave="all", tally=on_both):
         remote(src, dst, SENT[leave], RECV[name], device).start()
@@ -253,15 +267,21 @@
             block = jnp.concatenate([zero8, heads_of[k], zero8, zero16], axis=0)
             right[1, 0, COLS:ROWS, k * CH : (k + 1) * CH] = block.astype(BF16)
 
-    grad = None
     for k in range(3):
         tail = cot[...]
         if k > 0:
             tail = jnp.where(f + k < NF, cnext[k - 1].astype(F32), 0.0).astype(BF16)
         right[1, 0, 0:COLS, k * CH : (k + 1) * CH] = tail
-        term = dot_back(right[1, 0, :, k * CH : (k + 1) * CH], tw[k])
-        grad = term if grad is None else grad + term
-    send(right.at[1, 0], right.at[1, 1], "sib", sibling)
+
+    def act_grad(n):
+        acc = None
+        for k in range(3):
+            term = dot_back(right[1, 0, 0:n, k * CH : (k + 1) * CH], tw[k])
+            acc = term if acc is None else acc + term
+        grads[0:n] = acc
+        send(right.at[1, 0, pl.ds(0, n)], right.at[1, 1, pl.ds(0, n)], "sib", sibling, tally=on_rows[n])
+
+    by_rows(act_grad)
 
     pl.semaphore_wait(known.at[0], len(ring))
     further = [at_z(2), at_z(NZ - 2), at_y(2), at_y(NY - 2)]
@@ -294,28 +314,43 @@
 
     local(3, wv, wv).wait()
 
-    xs = left[:, 0 : 3 * CH]
-    pre = down(dot(xs, wv[0].reshape(3 * CH, CH)))
-    pre = pre + dot(xs, wv[1].reshape(3 * CH, CH))
-    pre = pre + up(dot(xs, wv[2].reshape(3 * CH, CH)))
-    pre = pre + vecs[1]
-    sig = jax.nn.sigmoid(pre)
-    left[:, 3 * CH : 4 * CH] = (pre * sig).astype(BF16)
-    slope = sig * (1.0 + pre * (1.0 - sig))
-
     half_other = pl.multiple_of(2 * CH * (1 - c), 2 * CH)
     half_mine = pl.multiple_of(2 * CH * c, 2 * CH)
-    send(left.at[:, pl.ds(half_other, 2 * CH)], lsib.at[1], "sib", sibling)
-
-    pg16 = (grad.astype(BF16).astype(F32) * slope).astype(BF16)
-    pg = pg16.astype(F32)
-    right[0, 0, :, CH : 2 * CH] = pg16
-    theirs = right.at[0, 1, :, pl.ds(CH, CH)]
-    send(right.at[0, 0, :, pl.ds(CH, CH)], theirs, "psib", sibling)
-    pgt[...] = pg16[0:COLS]
-    pg_own = pg[FIRST : FIRST + OWN]
-    pgh[...] = pg_own.astype(BF16)
-    pgb[...] = stacked(jnp.where(low, pg_own[OWN - HEAD :], pg_own[:HEAD]))
+
+    def theirs(n):
+        return right.at[0, 1, pl.ds(0, n), pl.ds(CH, CH)]
+
+    def terms(j, core, n):
+        return dot_outer(lsib[core, 0:n, j * CH : (j + 1) * CH], right[0 if j == 0 else c, core, 0:n])
+
+    def forward(n):
+        xs = left[0:n, 0 : 3 * CH]
+        pre = down(dot(xs, wv[0].reshape(3 * CH, CH)))
+        pre = pre + dot(xs, wv[1].reshape(3 * CH, CH))
+        pre = pre + up(dot(xs, wv[2].reshape(3 * CH, CH)))
+        pre = pre + vecs[1]
+        sig = jax.nn.sigmoid(pre)
+        left[0:n, 3 * CH : 4 * CH] = (pre * sig).astype(BF16)
+        slope = sig * (1.0 + pre * (1.0 - sig))
+        send(
+            left.at[pl.ds(0, n), pl.ds(half_other, 2 * CH)], lsib.at[1, pl.ds(0, n)], "sib", sibling, tally=on_rows[n]
+        )
+        pg16 = (grads[0:n].astype(BF16).astype(F32) * slope).astype(BF16)
+        pg = pg16.astype(F32)
+        right[0, 0, 0:n, CH : 2 * CH] = pg16
+        send(right.at[0, 0, pl.ds(0, n), pl.ds(CH, CH)], theirs(n), "psib", sibling, tally=on_rows[n])
+        pgt[...] = pg16[0:COLS]
+        if n == ROWS:
+            pg_own = pg[FIRST : FIRST + OWN]
+            pgh[...] = pg_own.astype(BF16)
+            pgb[...] = stacked(jnp.where(low, pg_own[OWN - HEAD :], pg_own[:HEAD]))
+        right[0, 0, 0:n, 0:CH] = up(pg).astype(BF16)
+        right[0, 0, 0:n, 2 * CH : 3 * CH] = down(pg).astype(BF16)
+        bias_terms = jnp.sum(pg, axis=0, keepdims=True)
+        vec[0] = jnp.concatenate([bias_terms[:, 0:128], bias_terms[:, 128:256], jnp.zeros((2, 128), F32)], axis=0)
+        lsib[0, 0:n] = left[0:n, pl.ds(half_mine, 2 * CH)]
+
+    by_rows(forward)
 
     def head_rows(ro):
         i = 1 - ro
@@ -324,34 +359,12 @@
     def head_edge(ro):
         return remote(pgb, phb.at[1 - ro], SENT["ph0"] + 1 + ro, RECV["ph0"] + 1 - ro, (NF - 1 - f, at(0, ro)[1]))
 
-    for ro in (-1, 1):
-
-        @pl.when(row_ok(ro))
-        def _():
-            to_row(pgt, prow, "prow0", ro).start()
-
-        @pl.when(owner & row_ok(ro))
-        def _():
-            head_rows(ro).start()
-
-    for ro in (-1, 0, 1):
-
-        @pl.when(owner & row_ok(ro))
-        def _():
-            head_edge(ro).start()
-
-    right[0, 0, :, 0:CH] = up(pg).astype(BF16)
-    right[0, 0, :, 2 * CH : 3 * CH] = down(pg).astype(BF16)
-    bias_terms = jnp.sum(pg, axis=0, keepdims=True)
-    vec[0] = jnp.concatenate([bias_terms[:, 0:128], bias_terms[:, 128:256], jnp.zeros((2, 128), F32)], axis=0)
-
-    lsib[0] = left[:, pl.ds(half_mine, 2 * CH)]
-
-    def terms(j, core):
-        return dot_outer(lsib[core, :, j * CH : (j + 1) * CH], right[0 if j == 0 else c, core])
-
-    for j in range(2):
-        prod[j] = terms(j, 0)
+    def own_terms(n):
+        for j in range(2):
+            prod[j] = terms(j, 0, n)
+
+    by_rows(own_terms)
+
     def pair_of_taps(t, lanes=slice(0, CH)):
         parts = [
             prod[tap // 3, :, (tap % 3) * CH + lanes.start : (tap % 3) * CH + lanes.stop].reshape(NX, NZ, 8, -1)
@@ -365,23 +378,26 @@
             send(g.at[k, lax.rem(x + o, NX)], xb.at[k, o - 1], f"x{k}", at_x(o), tally=tally)
 
     def last_products():
-        prod[1] = prod[1] + terms(1, 1)
+        def add(n):
+            prod[1] = prod[1] + terms(1, 1, n)
+
+        by_rows(add)
 
     def by_z():
-        for i in range(3):
-            block = pair_of_taps((3 + i) // 2, HALVES[(3 + i) % 2])
+        for i in range(2):
+            block = pair_of_taps(2, HALVES[i])
             for j in range(NX):
                 gz[:, j, i] = block[j]
         for o in AROUND_8:
             send(gz.at[lax.rem(z + o, NZ)], zfb.at[o - 1], "last1", at_z(o), tally=on_0)
 
-    def by_y():
+    def by_y(i):
         for half in range(2):
-            gy[half * NX : (half + 1) * NX] = pair_of_taps(2, HALVES[half])
+            gy[i, half * NX : (half + 1) * NX] = pair_of_taps(1 + i, HALVES[half])
         for o in AROUND_8:
-            send(gy.at[lax.rem(y + o, NY)], yfb.at[o - 1], "last1", at_y(o), tally=on_1)
-
-    wait_arrived("sib", sizes.at[pl.ds(0, 140)])
+            send(gy.at[i, lax.rem(y + o, NY)], yfb.at[i, o - 1], OVER_Y[i][0], at_y(o), tally=on_1)
+
+    by_rows(lambda n: wait_arrived("sib", sizes.at[pl.ds(0, n * 5 // 8)]))
     pl.semaphore_wait(known.at[1], len(further))
     for o in AROUND_X:
         send(vec.at[0], vxb.at[o - 1], "vx", at_x(o), "vec")
@@ -389,27 +405,50 @@
     @pl.when(c == 1)
     def _():
         last_products()
-        by_y()
-
-    wait_arrived("psib", theirs)
-    other = right[0, 1, :, CH : 2 * CH].astype(F32)
-    right[0, 1, :, 0:CH] = up(other).astype(BF16)
-    right[0, 1, :, 2 * CH : 3 * CH] = down(other).astype(BF16)
-
-    prod[0] = prod[0] + terms(0, 1)
+        by_y(1)
+
+    def add_first(n):
+        wait_arrived("psib", theirs(n))
+        other = right[0, 1, 0:n, CH : 2 * CH].astype(F32)
+        right[0, 1, 0:n, 0:CH] = up(other).astype(BF16)
+        right[0, 1, 0:n, 2 * CH : 3 * CH] = down(other).astype(BF16)
+        prod[0] = prod[0] + terms(0, 1, n)
+
+    by_rows(add_first)
+
+    @pl.when(c == 0)
+    def _():
+        last_products()
+        by_z()
+
     by_x(0)
     by_x(1)
 
     @pl.when(c == 0)
     def _():
-        last_products()
-        by_z()
-
-    by_x(2)
+        by_x(2, on_0)
+        by_x(3, on_0)
 
     @pl.when(c == 1)
     def _():
-        by_x(3, on_1)
+        by_y(0)
+
+
+    for ro in (-1, 1):
+
+        @pl.when(row_ok(ro))
+        def _():
+            to_row(pgt, prow, "prow0", ro).start()
+
+        @pl.when(owner & row_ok(ro))
+        def _():
+            head_rows(ro).start()
+
+    for ro in (-1, 0, 1):
+
+        @pl.when(owner & row_ok(ro))
+        def _():
+            head_edge(ro).start()
 
     def weight_rows(tap):
         both = wv[tap % 3, tap // 3, pl.ds(pl.multiple_of(16 * lax.div(r, 2), 16), 16), :].astype(F32)
@@ -448,13 +487,15 @@
         for o in AROUND_8:
             send(h.at[k, lax.rem(z + o, NZ)], zb.at[k, o - 1], f"z{k}", at_z(o), tally=tally)
 
-    for k in range(3):
+    for k in range(2):
         x_to_z(k)
 
     belongs = lax.rem(y, NX)
-
-    def to_its_row(i):
-        return remote(hy.at[i], rows_in.at[r], SENT["odd"], RECV["last2"], (f, belongs * NZ + i))
+    half_at = lax.div(y, NX)
+
+    def to_its_row(i, to_z):
+        _, arrive, _, leave = OVER_Y[i]
+        return remote(hy.at[i, to_z], rows_in.at[i, r], SENT[leave], RECV[arrive], (f, belongs * NZ + to_z))
 
     @pl.when(c == 0)
     def _():
@@ -462,22 +503,34 @@
         hx[...] = total_of(gz[z], zfb, NZ - 1).astype(BF16)
         for o in AROUND_X:
             send(hx.at[lax.rem(x + o, NX)], xlb.at[o - 1], "last2", at_x(o), tally=on_0)
+        x_to_z(2, on_0)
+        x_to_z(3, on_0)
 
     @pl.when(c == 1)
     def _():
-        x_to_z(3, on_1)
-        wait_arrived("last1", yfb)
-        hy[...] = total_of(gy[y], yfb, NY - 1).astype(BF16)
-        for i in range(NZ):
-
-            @pl.when((x != belongs) | (z != i))
+        for i in (1, 0):
+            wait_arrived(OVER_Y[i][0], yfb.at[i])
+            hy[i] = total_of(gy[i, y], yfb.at[i], NY - 1).astype(BF16)
+            for to_z in range(NZ):
+
+                @pl.when((x != belongs) | (z != to_z))
+                def _():
+                    to_its_row(i, to_z).start()
+
+            @pl.when(x == belongs)
             def _():
-                to_its_row(i).start()
-
-        @pl.when(x == belongs)
-        def _():
-            rows_in[r] = hy[z]
-
+                rows_in[i, r] = hy[i, z]
+
+    def z_to_y(k, tally=on_both):
+        wait_arrived(f"z{k}", zb.at[k])
+        over_y(k, total_of(h[k, z], zb.at[k], NZ - 1), tally)
+
+    def to_all(i, o):
+        _, _, arrive, leave = OVER_Y[i]
+        return remote(ends.at[i, half_at], ends.at[i, half_at], SENT[leave], RECV[arrive], at_y(o))
+
+    z_to_y(0)
+    z_to_y(1)
     for dr in (-1, 1):
         from_row(prow, "prow0", dr)
     for p in range(3):
@@ -497,7 +550,7 @@
             def _():
                 wait_arrived("ph0", sizes.at[pl.ds(0, 9 if dr else 1)], dr + 1)
 
-            own = pg_own if dr == 0 else phr[0 if dr < 0 else 1].astype(F32)
+            own = pgh[...].astype(F32) if dr == 0 else phr[0 if dr < 0 else 1].astype(F32)
             block = head_block(phb[dr + 1], own, phb[dr + 1])
             if dr != 0:
                 block = jnp.where(row_ok(dr), block, 0.0)
@@ -530,28 +583,35 @@
 
     local(0, gt_v, gt_o).start()
 
-    def z_to_y(k, tally=on_both):
-        wait_arrived(f"z{k}", zb.at[k])
-        over_y(k, total_of(h[k, z], zb.at[k], NZ - 1), tally)
-
-    def to_all(o):
-        half = lax.div(y, NX)
-        return remote(ends.at[half], ends.at[half], SENT["odd"], RECV["ends"], at_y(o))
-
-    z_to_y(0)
-    z_to_y(1)
-    z_to_y(2)
-
-    @pl.when(c == 1)
-    def _():
-        z_to_y(3, on_1)
-
     @pl.when(c == 0)
     def _():
+        z_to_y(2, on_0)
+        z_to_y(3, on_0)
         wait_arrived("last2", xlb)
         acc = total_of(hx[x], xlb, NX - 1)
-        for i in range(3):
-            over_y(3 + i, acc[i], on_0)
+        for i in range(2):
+            over_y(4 + i, acc[i], on_0)
+
+    @pl.when(c == 1)
+    def _():
+        for i in (1, 0):
+            _, arrive, _, leave = OVER_Y[i]
+
+            @pl.when(x != belongs)
+            def _():
+                wait_left(leave, NZ)
+
+            @pl.when(x == belongs)
+            def _():
+                wait_left(leave, NZ - 1)
+                wait_arrived(arrive, rows_in.at[i, pl.ds(0, NR - 1)])
+                acc = total_of(rows_in[i, 0], rows_in.at[i, pl.ds(1, NR - 1)], NR - 1)
+                ends[i, half_at] = acc
+                for o in AROUND_8:
+                    to_all(i, o).start()
+                lanes = pl.ds(pl.multiple_of(128 * half_at, 128), 128)
+                t = 2 * (1 + i)
+                psum[...] = psum[...] + (acc[0:8] * wsel[t, :, lanes] + acc[8:16] * wsel[t + 1, :, lanes])
 
     wait_arrived("vz", vzb)
     vec_left(vzb)
@@ -566,20 +626,6 @@
         for core in (c, 1 - c):
             send(vyb.at[f], vyb.at[f], "vy", (lax.rem(y + o, NY) * 2 + core, r), "vec")
     send(vyb.at[f], vyb.at[f], "vy", sibling, "vec")
-    @pl.when(c == 1)
-    def _():
-        @pl.when(x != belongs)
-        def _():
-            wait_left("odd", NZ)
-
-        @pl.when(x == belongs)
-        def _():
-            wait_left("odd", NZ - 1)
-            wait_arrived("last2", rows_in.at[pl.ds(0, NR - 1)])
-            ends[lax.div(y, NX)] = total_of(rows_in[0], rows_in.at[pl.ds(1, NR - 1)], NR - 1)
-            for o in AROUND_8:
-                to_all(o).start()
-
     wait_arrived("vy", vyb.at[pl.ds(0, NF - 1)])
     both = total_of(vyb[0], vyb.at[pl.ds(1, NF - 1)], NF - 1) * SCALE
     lower = r < NR // 2
@@ -608,35 +654,34 @@
 
     @pl.when(c == 1)
     def _():
-        wait_arrived("y", yb.at[pl.ds(0, NY - 1), pl.ds(0, 4)])
-
-        @pl.when(x == belongs)
-        def _():
-            wait_arrived("ends", ends.at[0])
-            wait_left("odd", 2 * (NY - 1))
-
-        @pl.when(x != belongs)
-        def _():
-            wait_arrived("ends", ends)
+        wait_arrived("y", yb.at[pl.ds(0, NY - 1), pl.ds(0, 2)])
+        for i in range(2):
+            _, _, arrive, leave = OVER_Y[i]
+
+            @pl.when(x == belongs)
+            def _():
+                wait_arrived(arrive, ends.at[i, 0])
+                wait_left(leave, 2 * (NY - 1))
+
+            @pl.when(x != belongs)
+            def _():
+                wait_arrived(arrive, ends.at[i])
 
     acc = total_of(yb[0], yb.at[pl.ds(1, NY - 1)], NY - 1)
     for t in range(3):
         both = jnp.concatenate([acc[2 * t], acc[2 * t + 1]], axis=1)
-        if t == 2:
-            both = jnp.where(c == 0, both, jnp.concatenate([ends[0], ends[1]], axis=1))
+        if t > 0:
+            both = jnp.where(c == 0, both, jnp.concatenate([ends[t - 1, 0], ends[t - 1, 1]], axis=1))
         total[2 * t : 2 * t + 2] = (both * SCALE).reshape(2, 8, CH)
     send(total, taps_o.at[pl.ds(6 * c, 6)], "total", sibling)
     local(3, total, taps_o.at[pl.ds(6 * c, 6)]).start()
     wait_arrived("total", total)
 
-    @pl.when(c == 0)
-    def _():
-        wait_left("all", sum(on_both) + sum(on_0))
-
-    @pl.when(c == 1)
-    def _():
-        wait_left("all", sum(on_both) + sum(on_1))
-
+    def all_left(n):
+        for core, more in ((0, on_0), (1, on_1)):
+            pl.when(c == core)(functools.partial(wait_left, "all", sum(on_both) + sum(more) + sum(on_rows[n])))
+
+    by_rows(all_left)
     vec_left(vyb.at[pl.ds(0, NF - 1)])
     for ro in (-1, 0, 1):
         @pl.when(row_ok(ro) if ro else f != mine_at)
@@ -676,12 +721,12 @@
         ((3, ROWS, CH), BF16), ((2, COLS, CH), BF16), ((COLS, CH), BF16), ((OWN, CH), BF16),
         ((16, 128), BF16), ((2, OWN, CH), BF16), ((3, 16, 128), BF16), ((NF // 2, 16, 128), BF16),
         ((16, 128), BF16), ((6, 8, CH), F32),
-        ((2, CH, 3 * CH), F32), ((4, NX, NZ, 16, 128), BF16), ((4, NX - 1, NZ, 16, 128), BF16),
+        ((ROWS, CH), F32), ((2, CH, 3 * CH), F32), ((4, NX, NZ, 16, 128), BF16), ((4, NX - 1, NZ, 16, 128), BF16),
         ((4, NZ, 16, 128), BF16), ((4, NZ - 1, 16, 128), BF16),
-        ((NZ, NX, 3, 16, 128), BF16), ((NZ - 1, NX, 3, 16, 128), BF16), ((NX, 3, 16, 128), BF16),
-        ((NX - 1, 3, 16, 128), BF16),
-        ((NY, NZ, 16, 128), BF16), ((NY - 1, NZ, 16, 128), BF16), ((NZ, 16, 128), BF16), ((NR, 16, 128), BF16),
-        ((2, 16, 128), F32), ((8, 128), F32), ((NY, 6, 16, 128), BF16),
+        ((NZ, NX, 2, 16, 128), BF16), ((NZ - 1, NX, 2, 16, 128), BF16), ((NX, 2, 16, 128), BF16),
+        ((NX - 1, 2, 16, 128), BF16),
+        ((2, NY, NZ, 16, 128), BF16), ((2, NY - 1, NZ, 16, 128), BF16), ((2, NZ, 16, 128), BF16),
+        ((2, NR, 16, 128), BF16), ((2, 2, 16, 128), F32), ((8, 128), F32), ((NY, 6, 16, 128), BF16),
         ((6, 8, CH), F32),
         ((2, 4, 128), F32), ((NZ - 1, 4, 128), F32), ((NX - 1, 4, 128), F32), ((NF, 4, 128), F32),
         ((UNITS, 8, 128), F32),

time: 43.1 us -> 42 us (0.974)
  Pallas kernels: 42.3 us -> 41.2 us
    pallas_call x1, Pallas kernels: 41.6 us -> 40.5 us  [body(): pl.pallas_call(kernel, out_shape=tuple((pltpu.VMEM(shape, kind) for shape...]
where the time goes in v5:
time: 42 us; the launch traced here: 41.8 us
  Pallas kernels  41.2 us (98%)
  between operations  0.64 us (2%)
    pallas_call x1, Pallas kernels, body(): pl.pallas_call(kernel, out_shape=tuple((pltpu.VMEM(shape, kind) for shape...  40.5 us

profile of v5, /device:TPU:1, one launch (start us, length us, event | category | flops | bytes accessed | tf_op | source)
XLA Modules:
  0.0 41.8 jit_solution(7146003677819101928)
XLA Ops:
  0.6 40.5 %video_block_backward.1 = (bf16[128,256]{1,0:T(8,128)(2,1)S(1)}, bf16[8,256]{1,0:T(8,128)(2,1)S(1)}, f32[12,8,256]{2,1,0:T(8,128)S(1)}, f32[2,8]{1,0:T(2,128)S(1)}) custom-call(bf16[128,256]{1,0:T(8,128)(2,1)} %bitcast.10, bf16[8,256]{1,0:T(8,128)(2,1)} %bitcast.12, bf16[128,256]{1,0:T(8,128)(2,1)} %bitcast.11, bf16[8,256]{1,0:T(8,128)(2,1)} %bitcast.13, ...), custom_call_target="tpu_custom_call" | custom-call | tf_op jit(solution)/shard_map/video_block_backward/pallas_call | solution.py:745
  41.1 0.7 %write_out.1 = (bf16[128,256]{1,0:T(8,128)(2,1)}, bf16[8,256]{1,0:T(8,128)(2,1)}, f32[9,8,256]{2,1,0:T(8,128)}, f32[3,8,256]{2,1,0:T(8,128)}, f32[2,8]{1,0:T(2,128)}) custom-call(bf16[128,256]{1,0:T(8,128)(2,1)S(1)} %get-tuple-element.14.gt, bf16[8,256]{1,0:T(8,128)(2,1)S(1)} %get-tuple-element.15.gh, f32[12,8,256]{2,1,0:T(8,128)S(1)} %get-tuple-element.16.taps, ...), custom_call_target="tpu_custom_call" | custom-call | tf_op jit(solution)/shard_map/write_out/pallas_call | solution.py:762

commit v6 on v5

--- a/solution.py
+++ b/solution.py
@@ -531,57 +531,6 @@
 
     z_to_y(0)
     z_to_y(1)
-    for dr in (-1, 1):
-        from_row(prow, "prow0", dr)
-    for p in range(3):
-        dr = 1 - p
-        if dr == 0:
-            rows = pgt[...]
-        else:
-            rows = prow[0 if dr < 0 else 1].astype(F32)
-            rows = jnp.where(row_ok(dr), rows, 0.0).astype(BF16)
-        back[p, 0:COLS, :] = rows
-
-    @pl.when(owner)
-    def _():
-        for p in range(3):
-            dr = 1 - p
-            @pl.when(row_ok(dr))
-            def _():
-                wait_arrived("ph0", sizes.at[pl.ds(0, 9 if dr else 1)], dr + 1)
-
-            own = pgh[...].astype(F32) if dr == 0 else phr[0 if dr < 0 else 1].astype(F32)
-            block = head_block(phb[dr + 1], own, phb[dr + 1])
-            if dr != 0:
-                block = jnp.where(row_ok(dr), block, 0.0)
-            back[p, COLS:ROWS, :] = block.astype(BF16)
-
-    convs = []
-    for q in range(3):
-        acc = None
-        for p in range(3):
-            term = dot_back(back[p], wv[q, p])
-            acc = term if acc is None else acc + term
-        convs.append(acc)
-    mod_grad = up(convs[0]) + convs[1] + down(convs[2])
-    tail_grad = mod_grad[0:COLS]
-    head_grad = mod_grad[FIRST : FIRST + OWN]
-    gt_v[...] = (cot[...].astype(F32) + modv * tail_grad).astype(BF16)
-
-    def head_result(o):
-        to = jnp.where(low, o, NF - 1 - o)
-        return remote(ghs.at[lax.rem(to, NF // 2)], ghr, SENT["ph1"], RECV["gh"], (to, r))
-
-    @pl.when(owner)
-    def _():
-        result = joined(chg, 0) + modv * head_grad
-        for k in range(OWN // HEAD):
-            ghs[k] = stacked(result[k * HEAD : (k + 1) * HEAD])
-        for o in range(1, NF // 2):
-            head_result(o).start()
-        ghr[...] = ghs[place]
-
-    local(0, gt_v, gt_o).start()
 
     @pl.when(c == 0)
     def _():
@@ -626,6 +575,58 @@
         for core in (c, 1 - c):
             send(vyb.at[f], vyb.at[f], "vy", (lax.rem(y + o, NY) * 2 + core, r), "vec")
     send(vyb.at[f], vyb.at[f], "vy", sibling, "vec")
+    for dr in (-1, 1):
+        from_row(prow, "prow0", dr)
+    for p in range(3):
+        dr = 1 - p
+        if dr == 0:
+            rows = pgt[...]
+        else:
+            rows = prow[0 if dr < 0 else 1].astype(F32)
+            rows = jnp.where(row_ok(dr), rows, 0.0).astype(BF16)
+        back[p, 0:COLS, :] = rows
+
+    @pl.when(owner)
+    def _():
+        for p in range(3):
+            dr = 1 - p
+            @pl.when(row_ok(dr))
+            def _():
+                wait_arrived("ph0", sizes.at[pl.ds(0, 9 if dr else 1)], dr + 1)
+
+            own = pgh[...].astype(F32) if dr == 0 else phr[0 if dr < 0 else 1].astype(F32)
+            block = head_block(phb[dr + 1], own, phb[dr + 1])
+            if dr != 0:
+                block = jnp.where(row_ok(dr), block, 0.0)
+            back[p, COLS:ROWS, :] = block.astype(BF16)
+
+    convs = []
+    for q in range(3):
+        acc = None
+        for p in range(3):
+            term = dot_back(back[p], wv[q, p])
+            acc = term if acc is None else acc + term
+        convs.append(acc)
+    mod_grad = up(convs[0]) + convs[1] + down(convs[2])
+    tail_grad = mod_grad[0:COLS]
+    head_grad = mod_grad[FIRST : FIRST + OWN]
+    gt_v[...] = (cot[...].astype(F32) + modv * tail_grad).astype(BF16)
+
+    def head_result(o):
+        to = jnp.where(low, o, NF - 1 - o)
+        return remote(ghs.at[lax.rem(to, NF // 2)], ghr, SENT["ph1"], RECV["gh"], (to, r))
+
+    @pl.when(owner)
+    def _():
+        result = joined(chg, 0) + modv * head_grad
+        for k in range(OWN // HEAD):
+            ghs[k] = stacked(result[k * HEAD : (k + 1) * HEAD])
+        for o in range(1, NF // 2):
+            head_result(o).start()
+        ghr[...] = ghs[place]
+
+    local(0, gt_v, gt_o).start()
+
     wait_arrived("vy", vyb.at[pl.ds(0, NF - 1)])
     both = total_of(vyb[0], vyb.at[pl.ds(1, NF - 1)], NF - 1) * SCALE
     lower = r < NR // 2

time: 42 us -> 42 us (level)
  no operation moved by 1% of the time
where the time goes in v6:
time: 42 us; the launch traced here: 41.9 us
  Pallas kernels  41.2 us (98%)
  between operations  0.64 us (2%)
    pallas_call x1, Pallas kernels, body(): pl.pallas_call(kernel, out_shape=tuple((pltpu.VMEM(shape, kind) for shape...  40.5 us

profile of v6, /device:TPU:1, one launch (start us, length us, event | category | flops | bytes accessed | tf_op | source)
XLA Modules:
  0.0 41.9 jit_solution(12142316882149961719)
XLA Ops:
  0.6 40.5 %video_block_backward.1 = (bf16[128,256]{1,0:T(8,128)(2,1)S(1)}, bf16[8,256]{1,0:T(8,128)(2,1)S(1)}, f32[12,8,256]{2,1,0:T(8,128)S(1)}, f32[2,8]{1,0:T(2,128)S(1)}) custom-call(bf16[128,256]{1,0:T(8,128)(2,1)} %bitcast.10, bf16[8,256]{1,0:T(8,128)(2,1)} %bitcast.12, bf16[128,256]{1,0:T(8,128)(2,1)} %bitcast.11, bf16[8,256]{1,0:T(8,128)(2,1)} %bitcast.13, ...), custom_call_target="tpu_custom_call" | custom-call | tf_op jit(solution)/shard_map/video_block_backward/pallas_call | solution.py:746
  41.1 0.7 %write_out.1 = (bf16[128,256]{1,0:T(8,128)(2,1)}, bf16[8,256]{1,0:T(8,128)(2,1)}, f32[9,8,256]{2,1,0:T(8,128)}, f32[3,8,256]{2,1,0:T(8,128)}, f32[2,8]{1,0:T(2,128)}) custom-call(bf16[128,256]{1,0:T(8,128)(2,1)S(1)} %get-tuple-element.14.gt, bf16[8,256]{1,0:T(8,128)(2,1)S(1)} %get-tuple-element.15.gh, f32[12,8,256]{2,1,0:T(8,128)S(1)} %get-tuple-element.16.taps, ...), custom_call_target="tpu_custom_call" | custom-call | tf_op jit(solution)/shard_map/write_out/pallas_call | solution.py:763
